TPU v7x, 256 devices: a whole 4x4x8 slice. The times are simulated.
256 devices in a mesh: tm: 4 (over y), ha: 16 (over z, core), wa: 4 (over x).
Axes of the slice: x: 4, y: 4, z: 8, core: 2. Of those that a mesh axis runs over, the one named last changes fastest.
Arguments:
- features: bfloat16 [4, 32, 512, 512], P('tm', 'ha', 'wa'), may hold values from -100 to 100
- gain_one: float32 [512], replicated, may hold values from 0.1 to 1.9
- shift_one: float32 [512], replicated, may hold values from -3 to 3
- conv_weight: bfloat16 [3, 3, 3, 512, 512], P(None, None, None, None, 'wa'), may hold values from -0.0546875 to 0.0546875
- gain_two: float32 [512], replicated, may hold values from 0.1 to 1.9
- shift_two: float32 [512], replicated, may hold values from -3 to 3
Outputs:
- block_out: bfloat16 [4, 32, 512, 512], P('tm', 'ha', 'wa')
All inputs are finite; a program needn't handle non-finite values.
Results may differ from a plain program's by a relative error of at most 0.012.
Values may be sent and summed in bfloat16 or wider, within the bound.
A program may use at most 128 MiB of HBM per device.

v0:
```python
import jax
import jax.numpy as jnp
from jax import lax
from jax.sharding import PartitionSpec as P

GROUPS = 32


def passed_along(value, axis, steps):
    count = lax.axis_size(axis)
    initial, last = (max(0, -steps), min(count, count - steps))
    return lax.ppermute(value, axis, [(source, source + steps) for source in range(initial, last)])


def extended(cells, sides, width):
    for axis, dim in sides:
        count = lax.axis_size(axis)
        ends = count - 1
        head = lax.slice_in_dim(cells, 0, width, axis=dim)
        tail = lax.slice_in_dim(cells, cells.shape[dim] - width, cells.shape[dim], axis=dim)
        cells = jnp.concatenate(
            [
                lax.ppermute(tail, axis, [(i, (i + 1) % count) for i in range(ends)]),
                cells,
                lax.ppermute(head, axis, [((i + 1) % count, i) for i in range(ends)]),
            ],
            axis=dim,
        )
    return cells


def normalize(values, gain_vector, offset_vector, entry_count):
    grouped = values.reshape(-1, GROUPS, values.shape[-1] // GROUPS)
    group_sum = lax.psum(jnp.sum(grouped, axis=(0, 2)), ("tm", "ha", "wa"))
    group_mean = group_sum / entry_count
    centered = grouped - group_mean[:, None]
    squared_sum = lax.psum(jnp.sum(centered * centered, axis=(0, 2)), ("tm", "ha", "wa"))
    group_var = squared_sum / entry_count
    scaled = centered * lax.rsqrt(group_var + 1e-06)[:, None]
    return scaled.reshape(values.shape) * gain_vector + offset_vector


def edge_fix(padded):
    ha_index = lax.axis_index("ha")
    last_row = lax.axis_size("ha") - 1
    top_rim = jnp.where(ha_index == 0, padded[:, 1:2], padded[:, 0:1])
    bottom = jnp.where(ha_index == last_row, padded[:, -2:-1], padded[:, -1:])
    padded = jnp.concatenate([top_rim, padded[:, 1:-1], bottom], axis=1)
    wa_index = lax.axis_index("wa")
    last_column = lax.axis_size("wa") - 1
    left_rim = jnp.where(wa_index == 0, padded[:, :, 1:2], padded[:, :, 0:1])
    right_rim = jnp.where(wa_index == last_column, padded[:, :, -2:-1], padded[:, :, -1:])
    return jnp.concatenate([left_rim, padded[:, :, 1:-1], right_rim], axis=2)


def apply_taps(stacks, kernel, height, columns):
    block_count = stacks.shape[0]
    row_total = block_count * height * columns
    running = jnp.zeros((row_total, kernel.shape[4]), jnp.float32)
    for depth_tap in range(3):
        for row_tap in range(3):
            for col_tap in range(3):
                window = stacks[
                    :, depth_tap, row_tap : row_tap + height, col_tap : col_tap + columns
                ].reshape(row_total, stacks.shape[-1])
                running = running + jnp.dot(
                    window, kernel[depth_tap, row_tap, col_tap], preferred_element_type=jnp.float32
                )
    return running.reshape(block_count, height * columns, kernel.shape[4])


def per_device(features, gain_one, shift_one, conv_weight, gain_two, shift_two):
    height = features.shape[1]
    columns = features.shape[2]
    channels = features.shape[3]
    cell_count = height * columns
    entry_count = (
        lax.axis_size("tm")
        * lax.axis_size("ha")
        * lax.axis_size("wa")
        * cell_count
        * (channels // GROUPS)
    )
    activated = jax.nn.silu(
        normalize(features.astype(jnp.float32), gain_one, shift_one, entry_count)
    ).astype(jnp.bfloat16)
    time_index = lax.axis_index("tm")
    carried = activated
    earlier = []
    for hop_index in range(2):
        carried = passed_along(carried, "tm", 1)
        earlier.append(carried)
    near_frame = jnp.where(time_index >= 1, earlier[0], activated)
    far_frame = jnp.where(time_index >= 2, earlier[1], near_frame)
    frame_stack = jnp.concatenate([far_frame, near_frame, activated], axis=0)
    padded = edge_fix(extended(frame_stack, (("ha", 1), ("wa", 2)), 1))
    convolved = apply_taps(
        padded[None], lax.all_gather(conv_weight, "wa", axis=4, tiled=True), height, columns
    )[0]
    convolved = convolved.reshape(1, height, columns, channels)
    return jax.nn.silu(normalize(convolved, gain_two, shift_two, entry_count)).astype(jnp.bfloat16)


def solution(mesh):
    in_specs = (P("tm", "ha", "wa", None), P(), P(), P(None, None, None, None, "wa"), P(), P())
    out_specs = P("tm", "ha", "wa", None)
    return jax.shard_map(
        per_device, mesh=mesh, in_specs=in_specs, out_specs=out_specs, check_vma=False
    )
```

profile of v0, /device:TPU:1, one launch (start us, length us, event | category | flops | bytes accessed | tf_op | source)
XLA Modules:
  0.0 388.3 jit_solution(5279232009626071383)
XLA Ops:
  6.5 0.7 all-gather.2.cloned.1.call-update
  7.3 1.0 convert_reduce_fusion
  8.3 0.1 reduce_sum.51
  8.5 82.1 %psum.28 = f32[32]{0:T(128)S(1)} all-reduce(f32[32]{0:T(128)S(1)} %reduce_sum.51), channel_id=1, replica_groups=mesh['tm'=4,'ha'=16,'wa'=4] {'tm','ha','wa'}, use_global_device_ids=true, to_apply=%region_2.0 | all-reduce | flops 32 | bytes 256 | tf_op jit(solution)/shard_map/psum | solution.py:34
  90.6 0.1 sub.41
  90.7 1.0 fusion.2
  91.8 0.1 reduce_sum.54
  91.9 73.3 %psum.29 = f32[32]{0:T(128)S(1)} all-reduce(f32[32]{0:T(128)S(1)} %reduce_sum.54), channel_id=1, replica_groups=mesh['tm'=4,'ha'=16,'wa'=4] {'tm','ha','wa'}, use_global_device_ids=true, to_apply=%region_5.6 | all-reduce | flops 32 | bytes 256 | tf_op jit(solution)/shard_map/psum | solution.py:37
  165.3 0.1 mul.87
  165.4 1.2 fusion.10
  166.5 2.6 collective-permute-start
  169.2 4.9 %collective-permute-done = bf16[1,2,128,512]{3,2,1,0:T(8,128)(2,1)S(1)} collective-permute-done((bf16[1,2,128,512]{3,2,1,0:T(8,128)(2,1)S(1)}, bf16[1,2,128,512]{3,2,1,0:T(8,128)(2,1)S(1)}, u32[]{:S(2)}, u32[]{:S(2)}) %collective-permute-start) | collective-permute-done | bytes 262176 | tf_op jit(solution)/shard_map/ppermute | solution.py:12
  174.1 4.1 %collective-permute-start.1 = (bf16[1,2,128,512]{3,2,1,0:T(8,128)(2,1)S(1)}, bf16[1,2,128,512]{3,2,1,0:T(8,128)(2,1)S(1)}, u32[]{:S(2)}, u32[]{:S(2)}) collective-permute-start(bf16[1,2,128,512]{3,2,1,0:T(8,128)(2,1)S(1)} %collective-permute-done), channel_id=1, source_target_pairs={{0,64},{64,128},{128,192},{1,65},{65,129},{129,193},{2,66},{66,130... | collective-permute-start | bytes 786440 | tf_op jit(solution)/shard_map/ppermute | solution.py:12
  178.2 4.0 %collective-permute-done.1 = bf16[1,2,128,512]{3,2,1,0:T(8,128)(2,1)S(1)} collective-permute-done((bf16[1,2,128,512]{3,2,1,0:T(8,128)(2,1)S(1)}, bf16[1,2,128,512]{3,2,1,0:T(8,128)(2,1)S(1)}, u32[]{:S(2)}, u32[]{:S(2)}) %collective-permute-start.1) | collective-permute-done | bytes 262176 | tf_op jit(solution)/shard_map/ppermute | solution.py:12
  182.2 1.2 broadcast_select_fusion.1
  183.5 0.1 pad_maximum_fusion.2
  183.7 6.0 %collective-permute-start.2 = (bf16[3,1,128,512]{3,2,1,0:T(8,128)(2,1)S(1)}, bf16[3,1,128,512]{3,2,1,0:T(8,128)(2,1)S(1)}, u32[]{:S(2)}, u32[]{:S(2)}) collective-permute-start(bf16[3,1,128,512]{3,2,1,0:T(8,128)(2,1)S(1)} %get-tuple-element.40), channel_id=1, source_target_pairs={{0,4},{4,8},{8,12},{12,16},{16,20},{20,24},{24,28},{28,32},{32,36}... | collective-permute-start | bytes 1179656 | tf_op jit(solution)/shard_map/ppermute | solution.py:23
  189.7 1.9 collective-permute-start.3
  191.6 2.8 collective-permute-done.2
  194.4 4.4 %collective-permute-done.3 = bf16[3,1,128,512]{3,2,1,0:T(8,128)(2,1)S(1)} collective-permute-done((bf16[3,1,128,512]{3,2,1,0:T(8,128)(2,1)S(1)}, bf16[3,1,128,512]{3,2,1,0:T(8,128)(2,1)S(1)}, u32[]{:S(2)}, u32[]{:S(2)}) %collective-permute-start.3) | collective-permute-done | bytes 393248 | tf_op jit(solution)/shard_map/ppermute | solution.py:25
  198.8 1.7 collective-permute-start.4
  200.5 1.3 collective-permute-start.5
  201.8 3.3 collective-permute-done.5
  205.1 0.9 pad_maximum_fusion
  206.0 0.1 slice_select_fusion.1
  206.1 0.2 pad_maximum_fusion.1
  206.3 0.4 slice.279
  206.8 0.6 maximum_bitcast_fusion
  207.4 1.4 fusion.13
  208.8 1.9 fusion.12
  210.7 1.6 fusion.11
  212.2 2.1 convolution_add_fusion.25
  214.3 2.2 convolution_add_fusion.24
  216.5 1.4 convolution_add_fusion.23
  218.0 1.4 convolution_add_fusion.22
  219.4 1.4 convolution_add_fusion.21
  220.8 1.4 convolution_add_fusion.20
  222.3 1.4 convolution_add_fusion.19
  223.7 1.2 convolution_add_fusion.18
  225.0 0.3 convolution_add_fusion.17
  225.3 0.3 convolution_add_fusion.16
  225.6 0.3 convolution_add_fusion.15
  226.0 0.3 convolution_add_fusion.14
  226.3 0.3 convolution_add_fusion.13
  226.6 0.3 convolution_add_fusion.12
  226.9 0.3 convolution_add_fusion.11
  227.2 0.3 convolution_add_fusion.10
  227.5 0.3 convolution_add_fusion.9
  227.8 0.3 convolution_add_fusion.8
  228.1 0.3 convolution_add_fusion.7
  228.4 0.3 convolution_add_fusion.6
  228.7 0.3 convolution_add_fusion.5
  229.0 0.3 convolution_add_fusion.4
  229.4 0.3 convolution_add_fusion.3
  229.7 0.3 convolution_add_fusion.2
  230.0 0.3 convolution_add_fusion.1
  230.3 0.3 fusion.15
  230.7 0.1 reduce_sum.72
  230.8 75.8 %psum.30 = f32[32]{0:T(128)S(1)} all-reduce(f32[32]{0:T(128)S(1)} %reduce_sum.72), channel_id=1, replica_groups=mesh['tm'=4,'ha'=16,'wa'=4] {'tm','ha','wa'}, use_global_device_ids=true, to_apply=%region_8.9 | all-reduce | flops 32 | bytes 256 | tf_op jit(solution)/shard_map/psum | solution.py:34
  306.7 0.1 sub.45
  306.8 0.1 multiply_reduce_fusion
  306.9 0.1 reduce_sum.75
  307.1 73.4 %psum.31 = f32[32]{0:T(128)S(1)} all-reduce(f32[32]{0:T(128)S(1)} %reduce_sum.75), channel_id=1, replica_groups=mesh['tm'=4,'ha'=16,'wa'=4] {'tm','ha','wa'}, use_global_device_ids=true, to_apply=%region_11.12 | all-reduce | flops 32 | bytes 256 | tf_op jit(solution)/shard_map/psum | solution.py:37
  380.6 0.9 multiply_convert_fusion
  (36 shorter events, 1.0 us)
Async XLA Ops:
  6.5 204.1 %all-gather.2.cloned.1.call-start = ((), (), s32[]{:S(2)}) async-start(), calls=%async_computation | async-start | bytes 17694720 | tf_op jit(solution)/shard_map/all_gather | solution.py:98
  166.5 7.6 %collective-permute-start = (bf16[1,2,128,512]{3,2,1,0:T(8,128)(2,1)S(1)}, bf16[1,2,128,512]{3,2,1,0:T(8,128)(2,1)S(1)}, u32[]{:S(2)}, u32[]{:S(2)}) collective-permute-start(bf16[1,2,128,512]{3,2,1,0:T(8,128)(2,1)S(1)} %fusion.10), channel_id=1, source_target_pairs={{0,64},{64,128},{128,192},{1,65},{65,129},{129,193},{2,66},{66,130... | collective-permute-start | bytes 786440 | tf_op jit(solution)/shard_map/ppermute | solution.py:12
  174.1 8.1 %collective-permute-start.1 = (bf16[1,2,128,512]{3,2,1,0:T(8,128)(2,1)S(1)}, bf16[1,2,128,512]{3,2,1,0:T(8,128)(2,1)S(1)}, u32[]{:S(2)}, u32[]{:S(2)}) collective-permute-start(bf16[1,2,128,512]{3,2,1,0:T(8,128)(2,1)S(1)} %collective-permute-done), channel_id=1, source_target_pairs={{0,64},{64,128},{128,192},{1,65},{65,129},{129,193},{2,66},{66,130... | collective-permute-start | bytes 786440 | tf_op jit(solution)/shard_map/ppermute | solution.py:12
  183.7 10.7 %collective-permute-start.2 = (bf16[3,1,128,512]{3,2,1,0:T(8,128)(2,1)S(1)}, bf16[3,1,128,512]{3,2,1,0:T(8,128)(2,1)S(1)}, u32[]{:S(2)}, u32[]{:S(2)}) collective-permute-start(bf16[3,1,128,512]{3,2,1,0:T(8,128)(2,1)S(1)} %get-tuple-element.40), channel_id=1, source_target_pairs={{0,4},{4,8},{8,12},{12,16},{16,20},{20,24},{24,28},{28,32},{32,36}... | collective-permute-start | bytes 1179656 | tf_op jit(solution)/shard_map/ppermute | solution.py:23
  189.7 9.1 %collective-permute-start.3 = (bf16[3,1,128,512]{3,2,1,0:T(8,128)(2,1)S(1)}, bf16[3,1,128,512]{3,2,1,0:T(8,128)(2,1)S(1)}, u32[]{:S(2)}, u32[]{:S(2)}) collective-permute-start(bf16[3,1,128,512]{3,2,1,0:T(8,128)(2,1)S(1)} %get-tuple-element.41), channel_id=1, source_target_pairs={{4,0},{8,4},{12,8},{16,12},{20,16},{24,20},{28,24},{32,28},{36,32}... | collective-permute-start | bytes 1179656 | tf_op jit(solution)/shard_map/ppermute | solution.py:25
  198.8 3.0 collective-permute-start.4
  200.5 4.6 %collective-permute-start.5 = (bf16[3,4,1,512]{3,2,1,0:T(2,128)(2,1)S(1)}, bf16[3,4,1,512]{3,2,1,0:T(2,128)(2,1)S(1)}, u32[]{:S(2)}, u32[]{:S(2)}) collective-permute-start(bf16[3,4,1,512]{3,2,1,0:T(2,128)(2,1)S(1)} %get-tuple-element.39), channel_id=1, source_target_pairs={{1,0},{2,1},{3,2},{5,4},{6,5},{7,6},{9,8},{10,9},{11,10},{13,12},{... | collective-permute-start | bytes 36872 | tf_op jit(solution)/shard_map/ppermute | solution.py:25
  210.6 13.1 %copy-start = (bf16[3,3,3,512,512]{4,3,2,1,0:T(8,128)(2,1)S(1)}, bf16[3,3,3,512,512]{4,3,2,1,0:T(8,128)(2,1)}, u32[]{:S(2)}) copy-start(bf16[3,3,3,512,512]{4,3,2,1,0:T(8,128)(2,1)} %all-gather.2.cloned.1.call-done) | copy-start | bytes 42467332
  210.6 14.3 %copy-start.4 = (bf16[1,1,2,128,512]{4,3,2,1,0:T(8,128)(2,1)S(1)}, bf16[1,1,2,128,512]{4,3,2,1,0:T(8,128)(2,1)}, u32[]{:S(2)}) copy-start(bf16[1,1,2,128,512]{4,3,2,1,0:T(8,128)(2,1)} %get-tuple-element.24) | copy-start | bytes 786436
  210.6 14.6 %copy-start.3 = (bf16[1,1,2,128,512]{4,3,2,1,0:T(8,128)(2,1)S(1)}, bf16[1,1,2,128,512]{4,3,2,1,0:T(8,128)(2,1)}, u32[]{:S(2)}) copy-start(bf16[1,1,2,128,512]{4,3,2,1,0:T(8,128)(2,1)} %get-tuple-element.23) | copy-start | bytes 786436
  210.6 15.0 %copy-start.2 = (bf16[1,1,2,128,512]{4,3,2,1,0:T(8,128)(2,1)S(1)}, bf16[1,1,2,128,512]{4,3,2,1,0:T(8,128)(2,1)}, u32[]{:S(2)}) copy-start(bf16[1,1,2,128,512]{4,3,2,1,0:T(8,128)(2,1)} %get-tuple-element.22) | copy-start | bytes 786436
  210.7 15.3 %copy-start.1 = (bf16[1,1,2,128,512]{4,3,2,1,0:T(8,128)(2,1)S(1)}, bf16[1,1,2,128,512]{4,3,2,1,0:T(8,128)(2,1)}, u32[]{:S(2)}) copy-start(bf16[1,1,2,128,512]{4,3,2,1,0:T(8,128)(2,1)} %get-tuple-element.21) | copy-start | bytes 786436
  225.6 4.7 %copy-start.5 = (bf16[1,1,2,128,512]{4,3,2,1,0:T(8,128)(2,1)S(1)}, bf16[1,1,2,128,512]{4,3,2,1,0:T(8,128)(2,1)}, u32[]{:S(2)}) copy-start(bf16[1,1,2,128,512]{4,3,2,1,0:T(8,128)(2,1)} %get-tuple-element.7) | copy-start | bytes 786436
  225.9 154.7 %copy-start.6 = (f32[512]{0:T(512)S(1)}, f32[512]{0:T(512)}, u32[]{:S(2)}) copy-start(f32[512]{0:T(512)} %param.11) | copy-start | bytes 6148
  225.9 154.7 %copy-start.7 = (f32[512]{0:T(512)S(1)}, f32[512]{0:T(512)}, u32[]{:S(2)}) copy-start(f32[512]{0:T(512)} %param.10) | copy-start | bytes 6148
Sparse Core Ops, SparseCore 0:
  9.2 142.7 all-gather.1
where the time goes:
time: 389 us; the launch traced here: 388 us
  blocking collectives  305 us (78%)
  waiting for transfers between devices  20.1 us (5%)
  matrix products  19.6 us (5%)
  starting transfers between devices  17.6 us (5%)
  between operations  13.9 us (4%)
  other arithmetic  7.89 us (2%)
  local copies, waits for them, and re-layouts  4.73 us (1%)
    psum x2, blocking collectives, normalize(): group_sum = lax.psum(jnp.sum(grouped, axis=(0, 2)), ('tm', 'ha', 'wa'))  158 us
    psum x2, blocking collectives, normalize(): lax.psum(jnp.sum(centered * centered, axis=(0, 2)), ('tm', 'ha', 'wa'))  147 us
    dot_general x27, matrix products, apply_taps(): jnp.dot(window, kernel[depth_tap, row_tap, col_tap], preferred_element_ty...  19.6 us
    ppermute x2, waiting for transfers between devices, passed_along(): lax.ppermute(value, axis, [(source, source + steps) for source in range(i...  8.95 us
  transfers between devices with their start and end apart: 7, of which 5 were waited for; matrix products, arithmetic and copies ran while one was open for 3% of the time, Pallas kernels for 0%

commit v1 on v0

v1 whole, which is shorter than its diff:
```python
import functools

import jax
import jax.numpy as jnp
from jax import lax
from jax.experimental import pallas as pl
from jax.experimental.pallas import tpu as pltpu
from jax.sharding import PartitionSpec as P

GROUPS = 32
LANES = 128
EPS = 1e-06
MESH = pl.DeviceIdType.MESH


def lane_blocks(rows):
    return [rows[k : k + 1, :] for k in range(rows.shape[0])]


def group_sum(values, width):
    axis = values.ndim - 1
    lane = lax.broadcasted_iota(jnp.int32, values.shape, axis)
    step = 1
    while step < width:
        ahead = pltpu.roll(values, step, axis)
        behind = pltpu.roll(values, LANES - step, axis)
        values = values + jnp.where((lane & step) != 0, ahead, behind)
        step *= 2
    return values


def combined(means, deviations, count, axis):
    mean = jnp.mean(means, axis=axis, keepdims=True)
    spread = means - mean
    total = jnp.sum(deviations, axis=axis) + count * jnp.sum(spread * spread, axis=axis)
    return jnp.squeeze(mean, axis), total


def group_norm_terms(mean, deviation, count, width):
    group_mean = group_sum(mean, width) / width
    spread = mean - group_mean
    group_var = group_sum(deviation + count * (spread * spread), width) / (count * width)
    return group_mean, lax.rsqrt(group_var + EPS)


def silu(v):
    half = 0.5 * v
    return half + half * jnp.tanh(half)


def kernel(
    nt, nh, nw,
    feat, gain_one, shift_one, weight, gain_two, shift_two, out,
    edge_out, blocks, edges, acts, pair_a, pair_b, rims, acc, conv, conv_out, rim_out, rim_in, back,
    plane_one, line_one, line_two, plane_two, norm, norm_edge,
    weight_sem, local_sem, send_sem, recv_sem, rim_send, rim_recv,
):
    t, h, w = lax.axis_index("tm"), lax.axis_index("ha"), lax.axis_index("wa")
    plane = nt * nw
    me = t * nw + w
    columns, channels = feat.shape[2], feat.shape[3]
    part = columns // nt
    blocks_of = channels // LANES
    width = channels // GROUPS
    depth = 3 * channels
    span = nw * part
    rows = nt * span
    entries = 2 * columns
    everywhere = entries * plane * nh

    def plane_id(j):
        return (lax.div(j, nw), h, lax.rem(j, nw))

    def plane_loop(body):
        def step(i, carry):
            body(lax.rem(me + i, plane))
            return carry

        lax.fori_loop(1, plane, step, 0)

    def line_loop(body):
        def step(i, carry):
            body(lax.rem(h + i, nh))
            return carry

        lax.fori_loop(1, nh, step, 0)

    barrier = pltpu.get_barrier_semaphore()

    def greet(device):
        pl.semaphore_signal(barrier, inc=1, device_id=device, device_id_type=MESH)

    plane_loop(lambda j: greet(plane_id(j)))
    line_loop(lambda j: greet((t, j, w)))

    above = jnp.where(h == 0, 0, 2)
    below = jnp.where(h == nh - 1, 2, 0)
    left_half, right_half = pl.ds(0, LANES), pl.ds(LANES, LANES)
    weight_copies = []
    for k in range(3):
        weight_copies += [
            (weight.at[k, above], rims.at[0, k]),
            (weight.at[k, below], rims.at[1, k]),
            (weight.at[k, 1], pair_a.at[k, :, left_half]),
            (weight.at[k, 0], pair_a.at[k, :, right_half]),
            (weight.at[k, 2], pair_b.at[k, :, left_half]),
            (weight.at[k, 1], pair_b.at[k, :, right_half]),
        ]
    weight_copies = [
        pltpu.make_async_copy(source, target, weight_sem.at[n])
        for n, (source, target) in enumerate(weight_copies)
    ]
    for copy in weight_copies:
        copy.start()

    values = feat[0].astype(jnp.float32)
    flat = values.reshape(entries, channels)
    mean = jnp.mean(flat, axis=0, keepdims=True)
    centered = flat - mean
    deviation = jnp.sum(centered * centered, axis=0, keepdims=True)
    plane_one[me] = jnp.zeros((8, LANES), jnp.float32)
    for k in range(blocks_of):
        lanes = slice(k * LANES, (k + 1) * LANES)
        plane_one[me, k : k + 1, :] = mean[:, lanes]
        plane_one[me, 4 + k : 5 + k, :] = deviation[:, lanes]
    for y in range(nt):
        left = (y * part - 1) % columns
        right = (y * part + part) % columns
        four = jnp.concatenate(
            [values[r, c : c + 1, :] for c in (left, right) for r in range(2)], axis=0
        )
        pieces = [four[:, k * LANES : (k + 1) * LANES] for k in range(blocks_of)]
        pieces += [jnp.zeros((4, LANES), jnp.float32)] * (4 - blocks_of)
        edge_out[y] = jnp.concatenate(pieces, axis=0).astype(jnp.bfloat16)

    own_block = pltpu.make_async_copy(feat.at[0, :, pl.ds(t * part, part), :], blocks.at[me], local_sem.at[0])
    own_edge = pltpu.make_async_copy(edge_out.at[t], edges.at[me], local_sem.at[1])
    own_block.start()
    own_edge.start()

    pl.semaphore_wait(barrier, plane - 1 + nh - 1)

    def remote(source, target, index, device):
        return pltpu.make_async_remote_copy(
            src_ref=source, dst_ref=target, send_sem=send_sem.at[index], recv_sem=recv_sem.at[index],
            device_id=device, device_id_type=MESH,
        )

    def all_arrived(buffer, index):
        pltpu.make_async_copy(buffer, buffer, recv_sem.at[index]).wait()

    def all_sent(buffer, index):
        pltpu.make_async_copy(buffer, buffer, send_sem.at[index]).wait()

    plane_loop(lambda j: remote(plane_one.at[me], plane_one.at[me], 0, plane_id(j)).start())

    def send_block(j):
        y = lax.div(j, nw)
        remote(feat.at[0, :, pl.ds(y * part, part), :], blocks.at[me], 1, plane_id(j)).start()
        remote(edge_out.at[y], edges.at[me], 2, plane_id(j)).start()

    plane_loop(send_block)

    others = pl.ds(0, plane - 1)
    all_arrived(plane_one.at[others], 0)
    all_sent(plane_one.at[others], 0)
    mean, deviation = combined(plane_one[:, 0:4, :], plane_one[:, 4:8, :], float(entries), 0)
    line_one[h] = jnp.concatenate([mean, deviation], axis=0)
    line_loop(lambda j: remote(line_one.at[h], line_one.at[h], 3, (t, j, w)).start())
    all_arrived(line_one.at[pl.ds(0, nh - 1)], 3)
    all_sent(line_one.at[pl.ds(0, nh - 1)], 3)
    mean, deviation = combined(line_one[:, 0:4, :], line_one[:, 4:8, :], float(entries * plane), 0)
    mean, inverse = group_norm_terms(mean, deviation, float(everywhere), float(width))
    wide_mean = jnp.concatenate(lane_blocks(mean[0:blocks_of]), axis=1)
    wide_scale = jnp.concatenate(lane_blocks(inverse[0:blocks_of]), axis=1) * gain_one[...]
    norm[0:1, :] = wide_mean
    norm[1:2, :] = wide_scale
    norm[2:3, :] = shift_one[...]
    for n, vector in enumerate((wide_mean, wide_scale, shift_one[...])):
        for k in range(blocks_of):
            norm_edge[n, 4 * k : 4 * k + 4, :] = jnp.broadcast_to(
                vector[:, k * LANES : (k + 1) * LANES], (4, LANES)
            )
        if blocks_of < 4:
            norm_edge[n, 4 * blocks_of :, :] = jnp.zeros((16 - 4 * blocks_of, LANES), jnp.float32)

    all_arrived(blocks.at[others], 1)
    all_arrived(edges.at[others], 2)
    own_block.wait()
    own_edge.wait()

    first = lax.broadcasted_iota(jnp.int32, (part, channels), 0) == 0
    last = lax.broadcasted_iota(jnp.int32, (part, channels), 0) == part - 1
    is_left = (lax.broadcasted_iota(jnp.int32, (16, LANES), 0) & 2) == 0

    def activate(j, carry):
        frame, block = lax.div(j, nw), lax.rem(j, nw)
        left_from = jnp.where(t == 0, jnp.maximum(block - 1, 0), block)
        right_from = jnp.where(t == nt - 1, jnp.minimum(block + 1, nw - 1), block)
        left_end = jnp.logical_and(t == 0, block == 0)
        right_end = jnp.logical_and(t == nt - 1, block == nw - 1)
        edge = jnp.where(
            is_left,
            edges[frame * nw + left_from].astype(jnp.float32),
            edges[frame * nw + right_from].astype(jnp.float32),
        )
        edge = silu((edge - norm_edge[0]) * norm_edge[1] + norm_edge[2])
        for r in range(2):
            middle = silu((blocks[j, r].astype(jnp.float32) - norm[0:1, :]) * norm[1:2, :] + norm[2:3, :])
            left = jnp.concatenate([edge[4 * k + r : 4 * k + r + 1] for k in range(blocks_of)], axis=1)
            right = jnp.concatenate([edge[4 * k + 2 + r : 4 * k + 3 + r] for k in range(blocks_of)], axis=1)
            left = jnp.where(left_end, middle[0:1, :], left)
            right = jnp.where(right_end, middle[part - 1 : part, :], right)
            before = jnp.where(first, left, pltpu.roll(middle, 1, 0)).astype(jnp.bfloat16)
            after = jnp.where(last, right, pltpu.roll(middle, part - 1, 0)).astype(jnp.bfloat16)
            middle = middle.astype(jnp.bfloat16)

            def put(slot, before=before, middle=middle, after=after, r=r):
                place = pl.ds(pl.multiple_of(slot * span + block * part, part), part)
                acts[r, place, 0:channels] = before
                acts[r, place, channels : 2 * channels] = middle
                acts[r, place, 2 * channels : 3 * channels] = after

            put(frame + 2)

            @pl.when(frame == 0)
            def _(put=put):
                put(0)
                put(1)

        return carry

    lax.fori_loop(0, plane, activate, 0)

    for copy in weight_copies:
        copy.wait()

    def window(r, k):
        return acts[r, pl.ds(pl.multiple_of(k * span, span), rows), :]

    for side in range(2):
        acc[:, left_half] = jnp.zeros((rows, LANES), jnp.float32)

        def rim_step(k, carry, side=side):
            acc[:, left_half] += jnp.dot(window(side, k), rims[side, k], preferred_element_type=jnp.float32)
            return carry

        lax.fori_loop(0, 3, rim_step, 0)
        rim_out[side] = acc[:, left_half].astype(jnp.bfloat16)

        at_end = (h == 0) if side == 0 else (h == nh - 1)

        @pl.when(at_end)
        def _(side=side):
            rim_in[side] = rim_out[side]

        @pl.when(jnp.logical_not(at_end))
        def _(side=side):
            pltpu.make_async_remote_copy(
                src_ref=rim_out.at[side], dst_ref=rim_in.at[1 - side],
                send_sem=rim_send.at[side], recv_sem=rim_recv.at[1 - side],
                device_id=(t, h - 1 if side == 0 else h + 1, w), device_id_type=MESH,
            ).start()

    acc[...] = jnp.zeros((rows, 2 * LANES), jnp.float32)

    def pair_step(k, carry):
        acc[...] += jnp.dot(window(0, k), pair_a[k], preferred_element_type=jnp.float32) + jnp.dot(
            window(1, k), pair_b[k], preferred_element_type=jnp.float32
        )
        return carry

    lax.fori_loop(0, 3, pair_step, 0)

    for side in range(2):
        at_end = (h == 0) if side == 0 else (h == nh - 1)

        @pl.when(jnp.logical_not(at_end))
        def _(side=side):
            pltpu.make_async_copy(rim_in.at[side], rim_in.at[side], rim_recv.at[side]).wait()
            pltpu.make_async_copy(rim_out.at[side], rim_out.at[side], rim_send.at[side]).wait()

    sums = jnp.zeros((1, LANES), jnp.float32)
    for r in range(2):
        total = acc[:, r * LANES : (r + 1) * LANES] + rim_in[r].astype(jnp.float32)
        conv[r] = total
        conv_out[r] = total.astype(jnp.bfloat16)
        sums = sums + jnp.sum(total, axis=0, keepdims=True)
    mean = sums / (2 * rows)
    deviation = jnp.zeros((1, LANES), jnp.float32)
    for r in range(2):
        centered = conv[r] - mean
        deviation = deviation + jnp.sum(centered * centered, axis=0, keepdims=True)
    line_two[h] = jnp.zeros((8, LANES), jnp.float32)
    line_two[h, 0:1, :] = mean
    line_two[h, 1:2, :] = deviation
    line_loop(lambda j: remote(line_two.at[h], line_two.at[h], 4, (t, j, w)).start())

    def block_rows(j):
        return conv_out.at[:, pl.ds(pl.multiple_of(j * part, part), part), :]

    own_place = back.at[:, pl.ds(t * part, part), pl.ds(pl.multiple_of(w * LANES, LANES), LANES)]
    plane_loop(lambda j: remote(block_rows(j), own_place, 5, plane_id(j)).start())
    own_back = pltpu.make_async_copy(block_rows(me), own_place, local_sem.at[0])
    own_back.start()

    all_arrived(line_two.at[pl.ds(0, nh - 1)], 4)
    all_sent(line_two.at[pl.ds(0, nh - 1)], 4)
    mean, deviation = combined(line_two[:, 0:1, :], line_two[:, 1:2, :], float(2 * rows), 0)
    plane_two[me] = jnp.zeros((8, LANES), jnp.float32)
    plane_two[me, 0:1, :] = mean
    plane_two[me, 1:2, :] = deviation
    plane_loop(lambda j: remote(plane_two.at[me], plane_two.at[me], 6, plane_id(j)).start())
    all_arrived(plane_two.at[others], 6)
    all_sent(plane_two.at[others], 6)
    gathered = plane_two[...].reshape(nt, nw, 8, LANES)
    mean, deviation = combined(gathered[:, :, 0, :], gathered[:, :, 1, :], float(2 * rows * nh), 0)
    mean, inverse = group_norm_terms(mean, deviation, float(everywhere), float(width))
    norm[0:1, :] = jnp.concatenate(lane_blocks(mean), axis=1)
    norm[1:2, :] = jnp.concatenate(lane_blocks(inverse), axis=1) * gain_two[...]
    norm[2:3, :] = shift_two[...]

    arrived_rows = conv_out.at[:, pl.ds(0, (plane - 1) * part), :]
    all_arrived(arrived_rows, 5)
    own_back.wait()
    for r in range(2):
        out[0, r] = silu(
            (back[r].astype(jnp.float32) - norm[0:1, :]) * norm[1:2, :] + norm[2:3, :]
        ).astype(jnp.bfloat16)

    all_sent(arrived_rows, 5)
    all_sent(blocks.at[others], 1)
    all_sent(edges.at[others], 2)


def solution(mesh):
    nt, nh, nw = mesh.shape["tm"], mesh.shape["ha"], mesh.shape["wa"]

    def per_device(features, gain_one, shift_one, conv_weight, gain_two, shift_two):
        columns, channels = features.shape[2], features.shape[3]
        own = conv_weight.shape[4]
        plane, part, depth = nt * nw, columns // nt, 3 * channels
        span = nw * part
        rows = nt * span
        vmem = pl.BlockSpec(memory_space=pltpu.VMEM)
        bf16, f32 = jnp.bfloat16, jnp.float32
        return pl.pallas_call(
            functools.partial(kernel, nt, nh, nw),
            out_shape=jax.ShapeDtypeStruct(features.shape, bf16),
            in_specs=[vmem, vmem, vmem, pl.BlockSpec(memory_space=pl.ANY), vmem, vmem],
            out_specs=vmem,
            scratch_shapes=[
                pltpu.VMEM((nt, 16, LANES), bf16),
                pltpu.VMEM((plane, 2, part, channels), bf16),
                pltpu.VMEM((plane, 16, LANES), bf16),
                pltpu.VMEM((2, (nt + 2) * span, depth), bf16),
                pltpu.VMEM((3, depth, 2 * own), bf16),
                pltpu.VMEM((3, depth, 2 * own), bf16),
                pltpu.VMEM((2, 3, depth, own), bf16),
                pltpu.VMEM((rows, 2 * own), f32),
                pltpu.VMEM((2, rows, own), f32),
                pltpu.VMEM((2, rows, own), bf16),
                pltpu.VMEM((2, rows, own), bf16),
                pltpu.VMEM((2, rows, own), bf16),
                pltpu.VMEM((2, columns, channels), bf16),
                pltpu.VMEM((plane, 8, LANES), f32),
                pltpu.VMEM((nh, 8, LANES), f32),
                pltpu.VMEM((nh, 8, LANES), f32),
                pltpu.VMEM((plane, 8, LANES), f32),
                pltpu.VMEM((8, channels), f32),
                pltpu.VMEM((3, 16, LANES), f32),
                pltpu.SemaphoreType.DMA((18,)),
                pltpu.SemaphoreType.DMA((2,)),
                pltpu.SemaphoreType.DMA((7,)),
                pltpu.SemaphoreType.DMA((7,)),
                pltpu.SemaphoreType.DMA((2,)),
                pltpu.SemaphoreType.DMA((2,)),
            ],
            compiler_params=pltpu.CompilerParams(
                collective_id=0, has_side_effects=True, vmem_limit_bytes=48 * 1024 * 1024
            ),
        )(
            features,
            gain_one.reshape(1, channels),
            shift_one.reshape(1, channels),
            conv_weight.reshape(3, 3, depth, own),
            gain_two.reshape(1, channels),
            shift_two.reshape(1, channels),
        )

    in_specs = (P("tm", "ha", "wa", None), P(), P(), P(None, None, None, None, "wa"), P(), P())
    return jax.shard_map(
        per_device, mesh=mesh, in_specs=in_specs, out_specs=P("tm", "ha", "wa", None), check_vma=False
    )
```

time: 389 us -> 53.6 us (0.14)
  blocking collectives: 305 us -> 0 us
  Pallas kernels: 0 us -> 47 us
  waiting for transfers between devices: 20.1 us -> 0 us
  matrix products: 19.6 us -> 0 us
  starting transfers between devices: 17.6 us -> 0 us
  between operations: 13.9 us -> 0.02 us
  other arithmetic: 7.89 us -> 0 us
    psum x4 -> x0, blocking collectives: 305 us -> none  [the longest x2 158 us: normalize(): group_sum = lax.psum(jnp.sum(grouped, axis=(0, 2)), ('tm', 'ha', 'wa'))]
    pallas_call x0 -> x1, Pallas kernels: none -> 47 us  [per_device(): pl.pallas_call(functools.partial(kernel, nt, nh, nw), out_shape=jax.Shape...]
    dot_general x27 -> x0, matrix products: 19.6 us -> none  [apply_taps(): jnp.dot(window, kernel[depth_tap, row_tap, col_tap], preferred_element_ty...]
    ppermute x6 -> x0, waiting for transfers between devices: 19.4 us -> none  [the longest x2 8.95 us: passed_along(): lax.ppermute(value, axis, [(source, source + steps) for source in range(i...]
    ppermute x6 -> x0, starting transfers between devices: 17.6 us -> none  [the longest x2 7.65 us: extended(): lax.ppermute(tail, axis, [(i, (i + 1) % count) for i in range(ends)])]
    unnamed x16 -> x13, local copies, waits for them, and re-layouts: 0.04 us -> 6.38 us
  transfers between devices with their start and end apart: 7 -> 0, of which waited for: 5 -> 0; matrix products, arithmetic and copies ran while one was open for 3% -> 0% of each run, Pallas kernels for 0% -> 0%
where the time goes in v1:
time: 53.6 us; the launch traced here: 53.4 us
  Pallas kernels  47 us (88%)
  local copies, waits for them, and re-layouts  6.38 us (12%)
    pallas_call x1, Pallas kernels, per_device(): pl.pallas_call(functools.partial(kernel, nt, nh, nw), out_shape=jax.Shape...  47 us
    unnamed x13, local copies, waits for them, and re-layouts  6.38 us

profile of v1, /device:TPU:1, one launch (start us, length us, event | category | flops | bytes accessed | tf_op | source)
XLA Modules:
  0.0 53.4 jit_solution(15998682553153926239)
XLA Ops:
  0.0 0.0 copy-start
  0.0 2.0 %copy-done = bf16[3,3,3,512,128]{4,3,2,1,0:T(8,128)(2,1)S(1)} copy-done((bf16[3,3,3,512,128]{4,3,2,1,0:T(8,128)(2,1)S(1)}, bf16[3,3,3,512,128]{4,3,2,1,0:T(8,128)(2,1)}, u32[]{:S(2)}) %copy-start) | copy-done | bytes 3538968
  2.0 0.0 copy-start.1
  2.0 0.9 %copy-done.1 = bf16[1,2,128,512]{3,2,1,0:T(8,128)(2,1)S(1)} copy-done((bf16[1,2,128,512]{3,2,1,0:T(8,128)(2,1)S(1)}, bf16[1,2,128,512]{3,2,1,0:T(8,128)(2,1)}, u32[]{:S(2)}) %copy-start.1) | copy-done | bytes 262168
  3.0 0.0 copy-start.2
  3.0 0.7 %copy-done.2 = f32[512]{0:T(512)S(1)} copy-done((f32[512]{0:T(512)S(1)}, f32[512]{0:T(512)}, u32[]{:S(2)}) %copy-start.2) | copy-done | bytes 2072
  3.6 0.0 copy-start.3
  3.6 0.7 %copy-done.3 = f32[512]{0:T(512)S(1)} copy-done((f32[512]{0:T(512)S(1)}, f32[512]{0:T(512)}, u32[]{:S(2)}) %copy-start.3) | copy-done | bytes 2072
  4.3 0.0 copy-start.4
  4.3 0.7 %copy-done.4 = f32[512]{0:T(512)S(1)} copy-done((f32[512]{0:T(512)S(1)}, f32[512]{0:T(512)}, u32[]{:S(2)}) %copy-start.4) | copy-done | bytes 2072
  5.0 0.0 copy-start.5
  5.0 0.7 %copy-done.5 = f32[512]{0:T(512)S(1)} copy-done((f32[512]{0:T(512)S(1)}, f32[512]{0:T(512)}, u32[]{:S(2)}) %copy-start.5) | copy-done | bytes 2072
  5.7 47.0 %shard_map.64 = bf16[1,2,128,512]{3,2,1,0:T(8,128)(2,1)S(1)} custom-call(bf16[1,2,128,512]{3,2,1,0:T(8,128)(2,1)S(1)} %copy-done.1, f32[1,512]{1,0:T(1,128)S(1)} %bitcast.6, f32[1,512]{1,0:T(1,128)S(1)} %bitcast.7, bf16[3,3,1536,128]{3,2,1,0:T(8,128)(2,1)S(1)} %bitcast.5, f32[1,512]{1,0:T(1,128)S(1)} %bitcast.8, f32[1,512]{1,0:T(1,128)S(1)} %bitcast.9), custom_call_target="tpu_custom_call" | custom-call | tf_op jit(solution)/shard_map/pallas_call | solution.py:347
  52.7 0.7 %copy.8 = bf16[1,2,128,512]{3,2,1,0:T(8,128)(2,1)} copy(bf16[1,2,128,512]{3,2,1,0:T(8,128)(2,1)S(1)} %shard_map.64) | data formatting | bytes 524288
Async XLA Ops:
  0.0 2.0 %copy-start = (bf16[3,3,3,512,128]{4,3,2,1,0:T(8,128)(2,1)S(1)}, bf16[3,3,3,512,128]{4,3,2,1,0:T(8,128)(2,1)}, u32[]{:S(2)}) copy-start(bf16[3,3,3,512,128]{4,3,2,1,0:T(8,128)(2,1)} %param.9) | copy-start | bytes 10616836
  2.0 0.9 %copy-start.1 = (bf16[1,2,128,512]{3,2,1,0:T(8,128)(2,1)S(1)}, bf16[1,2,128,512]{3,2,1,0:T(8,128)(2,1)}, u32[]{:S(2)}) copy-start(bf16[1,2,128,512]{3,2,1,0:T(8,128)(2,1)} %feat.1) | copy-start | bytes 786436
  3.0 0.7 %copy-start.2 = (f32[512]{0:T(512)S(1)}, f32[512]{0:T(512)}, u32[]{:S(2)}) copy-start(f32[512]{0:T(512)} %param.7) | copy-start | bytes 6148
  3.6 0.7 %copy-start.3 = (f32[512]{0:T(512)S(1)}, f32[512]{0:T(512)}, u32[]{:S(2)}) copy-start(f32[512]{0:T(512)} %param.8) | copy-start | bytes 6148
  4.3 0.7 %copy-start.4 = (f32[512]{0:T(512)S(1)}, f32[512]{0:T(512)}, u32[]{:S(2)}) copy-start(f32[512]{0:T(512)} %param.10) | copy-start | bytes 6148
  5.0 0.7 %copy-start.5 = (f32[512]{0:T(512)S(1)}, f32[512]{0:T(512)}, u32[]{:S(2)}) copy-start(f32[512]{0:T(512)} %param.11) | copy-start | bytes 6148

commit v2 on v1

v2 whole, which is shorter than its diff:
```python
import functools

import jax
import jax.numpy as jnp
from jax import lax
from jax.experimental import pallas as pl
from jax.experimental.pallas import tpu as pltpu
from jax.sharding import PartitionSpec as P

GROUPS = 32
LANES = 128
EPS = 1e-06
MESH = pl.DeviceIdType.MESH


def lane_blocks(rows):
    return [rows[k : k + 1, :] for k in range(rows.shape[0])]


def group_sum(values, width):
    axis = values.ndim - 1
    lane = lax.broadcasted_iota(jnp.int32, values.shape, axis)
    step = 1
    while step < width:
        ahead = pltpu.roll(values, step, axis)
        behind = pltpu.roll(values, LANES - step, axis)
        values = values + jnp.where((lane & step) != 0, ahead, behind)
        step *= 2
    return values


def combined(means, deviations, count, axis):
    mean = jnp.mean(means, axis=axis, keepdims=True)
    spread = means - mean
    total = jnp.sum(deviations, axis=axis) + count * jnp.sum(spread * spread, axis=axis)
    return jnp.squeeze(mean, axis), total


def group_norm_terms(mean, deviation, count, width):
    group_mean = group_sum(mean, width) / width
    spread = mean - group_mean
    group_var = group_sum(deviation + count * (spread * spread), width) / (count * width)
    return group_mean, lax.rsqrt(group_var + EPS)


def silu(v):
    half = 0.5 * v
    return half + half * jnp.tanh(half)


def hops(distance, count):
    return min(distance, count - distance)


def kernel(
    nt, nh, nw,
    feat_hbm, gain_one_hbm, shift_one_hbm, weight, gain_two_hbm, shift_two_hbm, out,
    feat, gain_one, shift_one, gain_two, shift_two,
    message, blocks, acts, pair_a, pair_b, rim_pair, rim_last, acc, conv, conv_out, rim_out, rim_in, back,
    plane_one, line_one, line_two, plane_two, norm, norm_edge,
    input_sem, weight_sem, local_sem, send_sem, recv_sem, rim_send, rim_recv,
):
    t, h, w = lax.axis_index("tm"), lax.axis_index("ha"), lax.axis_index("wa")
    plane = nt * nw
    me = t * nw + w
    columns, channels = feat.shape[2], feat.shape[3]
    part = columns // nt
    blocks_of = channels // LANES
    width = channels // GROUPS
    depth = 3 * channels
    span = nw * part
    rows = nt * span
    entries = 2 * columns
    everywhere = entries * plane * nh
    slots = sorted(range(nw), key=lambda d: d % 2)
    near = nw // 2
    offsets = [(a, b) for a in range(nt) for b in range(nw) if a or b]
    far_first = sorted(offsets, key=lambda d: -hops(d[0], nt) - hops(d[1], nw))

    def plane_peer(offset):
        return lax.rem(t + offset[0], nt), lax.rem(w + offset[1], nw)

    def line_loop(body):
        def step(i, carry):
            away = lax.div(i + 1, 2)
            offset = nh // 2 + jnp.where(lax.rem(i, 2) == 1, away, -away)
            body(lax.rem(h + offset, nh))
            return carry

        lax.fori_loop(0, nh - 1, step, 0)

    copy_in = [
        pltpu.make_async_copy(source, target, input_sem.at[n])
        for n, (source, target) in enumerate(
            (
                (feat_hbm, feat),
                (gain_one_hbm, gain_one),
                (shift_one_hbm, shift_one),
                (gain_two_hbm, gain_two),
                (shift_two_hbm, shift_two),
            )
        )
    ]
    copy_in[0].start()

    barrier = pltpu.get_barrier_semaphore()

    def greet(device):
        pl.semaphore_signal(barrier, inc=1, device_id=device, device_id_type=MESH)

    line_loop(lambda j: greet((t, j, w)))
    for offset in far_first:
        y, q = plane_peer(offset)
        greet((y, h, q))

    for copy in copy_in[1:]:
        copy.start()
    above = jnp.where(h == 0, 0, 2)
    below = jnp.where(h == nh - 1, 2, 0)
    left_half, right_half = pl.ds(0, LANES), pl.ds(LANES, LANES)
    weight_copies = []
    for side, row in ((0, above), (1, below)):
        weight_copies += [
            (weight.at[0, row], rim_pair.at[side, :, left_half]),
            (weight.at[1, row], rim_pair.at[side, :, right_half]),
            (weight.at[2, row], rim_last.at[side]),
        ]
    for k in range(3):
        weight_copies += [
            (weight.at[k, 1], pair_a.at[k, :, left_half]),
            (weight.at[k, 0], pair_a.at[k, :, right_half]),
            (weight.at[k, 2], pair_b.at[k, :, left_half]),
            (weight.at[k, 1], pair_b.at[k, :, right_half]),
        ]
    weight_copies = [
        pltpu.make_async_copy(source, target, weight_sem.at[n])
        for n, (source, target) in enumerate(weight_copies)
    ]

    copy_in[0].wait()
    for copy in weight_copies:
        copy.start()
    values = feat[0].astype(jnp.float32)
    flat = values.reshape(entries, channels)
    mean = jnp.mean(flat, axis=0, keepdims=True)
    centered = flat - mean
    deviation = jnp.sum(centered * centered, axis=0, keepdims=True)
    pieces = [mean[:, k * LANES : (k + 1) * LANES] for k in range(blocks_of)]
    pieces += [jnp.zeros((1, LANES), jnp.float32)] * (4 - blocks_of)
    pieces += [deviation[:, k * LANES : (k + 1) * LANES] for k in range(blocks_of)]
    pieces += [jnp.zeros((1, LANES), jnp.float32)] * (4 - blocks_of)
    local_terms = jnp.concatenate(pieces, axis=0)
    for y in range(nt):
        left = (y * part - 1) % columns
        right = (y * part + part) % columns
        four = jnp.concatenate(
            [values[r, c : c + 1, :] for c in (left, right) for r in range(2)], axis=0
        )
        pieces = [four[:, k * LANES : (k + 1) * LANES] for k in range(blocks_of)]
        pieces += [jnp.zeros((4, LANES), jnp.float32)] * (4 - blocks_of)
        message[y, 8:24, :] = jnp.concatenate(pieces, axis=0)
    line_one[h] = local_terms

    own_block = pltpu.make_async_copy(feat.at[0, :, pl.ds(t * part, part), :], blocks.at[me], local_sem.at[0])
    own_block.start()

    pl.semaphore_wait(barrier, plane - 1 + nh - 1)

    def remote(source, target, index, device):
        return pltpu.make_async_remote_copy(
            src_ref=source, dst_ref=target, send_sem=send_sem.at[index], recv_sem=recv_sem.at[index],
            device_id=device, device_id_type=MESH,
        )

    def all_arrived(buffer, index):
        pltpu.make_async_copy(buffer, buffer, recv_sem.at[index]).wait()

    def all_sent(buffer, index):
        pltpu.make_async_copy(buffer, buffer, send_sem.at[index]).wait()

    def send_blocks(stage):
        for offset in far_first:
            if (slots.index(offset[1]) >= near) == stage:
                y, q = plane_peer(offset)
                remote(feat.at[0, :, pl.ds(y * part, part), :], blocks.at[me], 1 + stage, (y, h, q)).start()

    line_loop(lambda j: remote(line_one.at[h], line_one.at[h], 3, (t, j, w)).start())
    send_blocks(0)
    others = pl.ds(0, plane - 1)
    all_arrived(line_one.at[pl.ds(0, nh - 1)], 3)
    mean, deviation = combined(line_one[:, 0:4, :], line_one[:, 4:8, :], float(entries), 0)
    combined_terms = jnp.concatenate([mean, deviation], axis=0)
    for y in range(nt):
        message[y, 0:8, :] = combined_terms
    for offset in far_first:
        y, q = plane_peer(offset)
        remote(message.at[y], plane_one.at[me], 0, (y, h, q)).start()
    send_blocks(1)
    plane_one[me] = message[t]
    for copy in copy_in[1:]:
        copy.wait()
    for copy in weight_copies:
        copy.wait()
    all_arrived(plane_one.at[others], 0)
    mean, deviation = combined(plane_one[:, 0:4, :], plane_one[:, 4:8, :], float(entries * nh), 0)
    mean, inverse = group_norm_terms(mean, deviation, float(everywhere), float(width))
    wide_mean = jnp.concatenate(lane_blocks(mean[0:blocks_of]), axis=1)
    wide_scale = jnp.concatenate(lane_blocks(inverse[0:blocks_of]), axis=1) * gain_one[...]
    norm[0:1, :] = wide_mean
    norm[1:2, :] = wide_scale
    norm[2:3, :] = shift_one[...]
    for n, vector in enumerate((wide_mean, wide_scale, shift_one[...])):
        for k in range(blocks_of):
            norm_edge[n, 4 * k : 4 * k + 4, :] = jnp.broadcast_to(
                vector[:, k * LANES : (k + 1) * LANES], (4, LANES)
            )
        if blocks_of < 4:
            norm_edge[n, 4 * blocks_of :, :] = jnp.zeros((16 - 4 * blocks_of, LANES), jnp.float32)

    first = lax.broadcasted_iota(jnp.int32, (part, channels), 0) == 0
    last = lax.broadcasted_iota(jnp.int32, (part, channels), 0) == part - 1
    is_left = (lax.broadcasted_iota(jnp.int32, (16, LANES), 0) & 2) == 0

    def activate(slot):
        block = lax.rem(w + slots[slot], nw)
        place = slice(slot * part, (slot + 1) * part)
        left_from = jnp.where(t == 0, jnp.maximum(block - 1, 0), block)
        right_from = jnp.where(t == nt - 1, jnp.minimum(block + 1, nw - 1), block)
        left_end = jnp.logical_and(t == 0, block == 0)
        right_end = jnp.logical_and(t == nt - 1, block == nw - 1)

        def step(frame, carry):
            edge = jnp.where(
                is_left, plane_one[frame * nw + left_from, 8:24, :], plane_one[frame * nw + right_from, 8:24, :]
            )
            edge = silu((edge - norm_edge[0]) * norm_edge[1] + norm_edge[2])
            for r in range(2):
                raw = blocks[frame * nw + block, r].astype(jnp.float32)
                middle = silu((raw - norm[0:1, :]) * norm[1:2, :] + norm[2:3, :])
                left = jnp.concatenate([edge[4 * k + r : 4 * k + r + 1] for k in range(blocks_of)], axis=1)
                right = jnp.concatenate([edge[4 * k + 2 + r : 4 * k + 3 + r] for k in range(blocks_of)], axis=1)
                left = jnp.where(left_end, middle[0:1, :], left)
                right = jnp.where(right_end, middle[part - 1 : part, :], right)
                before = jnp.where(first, left, pltpu.roll(middle, 1, 0)).astype(jnp.bfloat16)
                after = jnp.where(last, right, pltpu.roll(middle, part - 1, 0)).astype(jnp.bfloat16)
                middle = middle.astype(jnp.bfloat16)

                def put(moment, before=before, middle=middle, after=after, r=r):
                    acts[r, moment, place, 0:channels] = before
                    acts[r, moment, place, channels : 2 * channels] = middle
                    acts[r, moment, place, 2 * channels : 3 * channels] = after

                put(frame + 2)

                @pl.when(frame == 0)
                def _(put=put):
                    put(0)
                    put(1)

            return carry

        lax.fori_loop(0, nt, step, 0)

    def rim(side, stage, low, high):
        count = high - low
        window = acts[side, 2 : 2 + nt, low:high, :].reshape(nt * count, depth)
        early = jnp.dot(window, rim_pair[side], preferred_element_type=jnp.float32)
        late = jnp.dot(window, rim_last[side], preferred_element_type=jnp.float32)
        first_tap = early[:, 0:LANES].reshape(nt, count, LANES)
        second_tap = early[:, LANES:].reshape(nt, count, LANES)
        third_tap = late.reshape(nt, count, LANES)
        for frame in range(nt):
            total = first_tap[max(frame - 2, 0)] + second_tap[max(frame - 1, 0)] + third_tap[frame]
            rim_out[side, frame, low:high, :] = total.astype(jnp.bfloat16)
        at_end = h == jnp.where(side == 0, 0, nh - 1)

        @pl.when(at_end)
        def _():
            rim_in[side, :, low:high, :] = rim_out[side, :, low:high, :]

        @pl.when(jnp.logical_not(at_end))
        def _():
            pltpu.make_async_remote_copy(
                src_ref=rim_out.at[side, :, low:high, :], dst_ref=rim_in.at[1 - side, :, low:high, :],
                send_sem=rim_send.at[side, stage], recv_sem=rim_recv.at[1 - side, stage],
                device_id=(t, h - 1 + 2 * side, w), device_id_type=MESH,
            ).start()

    across = lax.rem(h, 2)
    for stage, (low, high) in enumerate(((0, near), (near, nw))):
        if stage == 0:
            all_arrived(blocks.at[pl.ds(0, nt * near - 1)], 1)
            own_block.wait()
        else:
            all_arrived(blocks.at[pl.ds(0, nt * (nw - near))], 2)
        for slot in range(low, high):
            activate(slot)
        rim(across, stage, low * part, high * part)
        rim(1 - across, stage, low * part, high * part)

    acc[...] = jnp.zeros((rows, 2 * LANES), jnp.float32)

    def pair_step(k, carry):
        acc[...] += jnp.dot(
            acts[0, pl.ds(k, nt)].reshape(rows, depth), pair_a[k], preferred_element_type=jnp.float32
        ) + jnp.dot(acts[1, pl.ds(k, nt)].reshape(rows, depth), pair_b[k], preferred_element_type=jnp.float32)
        return carry

    lax.fori_loop(0, 3, pair_step, 0)

    for side in range(2):
        at_end = (h == 0) if side == 0 else (h == nh - 1)

        @pl.when(jnp.logical_not(at_end))
        def _(side=side):
            for stage, (low, high) in enumerate(((0, near * part), (near * part, span))):
                into = rim_in.at[side, :, low:high, :]
                outof = rim_out.at[side, :, low:high, :]
                pltpu.make_async_copy(into, into, rim_recv.at[side, stage]).wait()
                pltpu.make_async_copy(outof, outof, rim_send.at[side, stage]).wait()

    sums = jnp.zeros((1, LANES), jnp.float32)
    for r in range(2):
        total = acc[:, r * LANES : (r + 1) * LANES] + rim_in[r].reshape(rows, LANES).astype(jnp.float32)
        conv[r] = total
        conv_out[r] = total.astype(jnp.bfloat16).reshape(nt, span, LANES)
        sums = sums + jnp.sum(total, axis=0, keepdims=True)
    mean = sums / (2 * rows)
    deviation = jnp.zeros((1, LANES), jnp.float32)
    for r in range(2):
        centered = conv[r] - mean
        deviation = deviation + jnp.sum(centered * centered, axis=0, keepdims=True)
    line_two[h] = jnp.zeros((8, LANES), jnp.float32)
    line_two[h, 0:1, :] = mean
    line_two[h, 1:2, :] = deviation
    line_loop(lambda j: remote(line_two.at[h], line_two.at[h], 4, (t, j, w)).start())

    own_place = back.at[:, pl.ds(t * part, part), pl.ds(pl.multiple_of(w * LANES, LANES), LANES)]
    for offset in far_first:
        y, q = plane_peer(offset)
        slot = slots.index(offset[1])
        remote(conv_out.at[:, y, slot * part : (slot + 1) * part, :], own_place, 5, (y, h, q)).start()
    own_back = pltpu.make_async_copy(conv_out.at[:, t, 0:part, :], own_place, local_sem.at[0])
    own_back.start()

    all_arrived(line_two.at[pl.ds(0, nh - 1)], 4)
    mean, deviation = combined(line_two[:, 0:1, :], line_two[:, 1:2, :], float(2 * rows), 0)
    plane_two[me] = jnp.zeros((8, LANES), jnp.float32)
    plane_two[me, 0:1, :] = mean
    plane_two[me, 1:2, :] = deviation
    for offset in far_first:
        y, q = plane_peer(offset)
        remote(plane_two.at[me], plane_two.at[me], 6, (y, h, q)).start()
    all_sent(plane_one.at[others], 0)
    all_sent(blocks.at[pl.ds(0, nt * near - 1)], 1)
    all_sent(blocks.at[pl.ds(0, nt * (nw - near))], 2)
    all_sent(line_one.at[pl.ds(0, nh - 1)], 3)
    all_sent(line_two.at[pl.ds(0, nh - 1)], 4)
    all_sent(blocks.at[others, :, :, 0:LANES], 5)
    all_arrived(blocks.at[others, :, :, 0:LANES], 5)
    own_back.wait()
    all_arrived(plane_two.at[others], 6)
    gathered = plane_two[...].reshape(nt, nw, 8, LANES)
    mean, deviation = combined(gathered[:, :, 0, :], gathered[:, :, 1, :], float(2 * rows * nh), 0)
    mean, inverse = group_norm_terms(mean, deviation, float(everywhere), float(width))
    norm[0:1, :] = jnp.concatenate(lane_blocks(mean), axis=1)
    norm[1:2, :] = jnp.concatenate(lane_blocks(inverse), axis=1) * gain_two[...]
    norm[2:3, :] = shift_two[...]
    for r in range(2):
        out[0, r] = silu(
            (back[r].astype(jnp.float32) - norm[0:1, :]) * norm[1:2, :] + norm[2:3, :]
        ).astype(jnp.bfloat16)
    all_sent(plane_two.at[others], 6)


def solution(mesh):
    nt, nh, nw = mesh.shape["tm"], mesh.shape["ha"], mesh.shape["wa"]

    def per_device(features, gain_one, shift_one, conv_weight, gain_two, shift_two):
        columns, channels = features.shape[2], features.shape[3]
        own = conv_weight.shape[4]
        plane, part, depth = nt * nw, columns // nt, 3 * channels
        span = nw * part
        rows = nt * span
        vmem = pl.BlockSpec(memory_space=pltpu.VMEM)
        bf16, f32 = jnp.bfloat16, jnp.float32
        return pl.pallas_call(
            functools.partial(kernel, nt, nh, nw),
            out_shape=pltpu.VMEM(features.shape, bf16),
            in_specs=[pl.BlockSpec(memory_space=pltpu.HBM)] * 6,
            out_specs=vmem,
            scratch_shapes=[
                pltpu.VMEM(features.shape, bf16),
                pltpu.VMEM((1, channels), f32),
                pltpu.VMEM((1, channels), f32),
                pltpu.VMEM((1, channels), f32),
                pltpu.VMEM((1, channels), f32),
                pltpu.VMEM((nt, 24, LANES), f32),
                pltpu.VMEM((plane, 2, part, channels), bf16),
                pltpu.VMEM((2, nt + 2, span, depth), bf16),
                pltpu.VMEM((3, depth, 2 * own), bf16),
                pltpu.VMEM((3, depth, 2 * own), bf16),
                pltpu.VMEM((2, depth, 2 * own), bf16),
                pltpu.VMEM((2, depth, own), bf16),
                pltpu.VMEM((rows, 2 * own), f32),
                pltpu.VMEM((2, rows, own), f32),
                pltpu.VMEM((2, nt, span, own), bf16),
                pltpu.VMEM((2, nt, span, own), bf16),
                pltpu.VMEM((2, nt, span, own), bf16),
                pltpu.VMEM((2, columns, channels), bf16),
                pltpu.VMEM((plane, 24, LANES), f32),
                pltpu.VMEM((nh, 8, LANES), f32),
                pltpu.VMEM((nh, 8, LANES), f32),
                pltpu.VMEM((plane, 8, LANES), f32),
                pltpu.VMEM((8, channels), f32),
                pltpu.VMEM((3, 16, LANES), f32),
                pltpu.SemaphoreType.DMA((5,)),
                pltpu.SemaphoreType.DMA((18,)),
                pltpu.SemaphoreType.DMA((1,)),
                pltpu.SemaphoreType.DMA((7,)),
                pltpu.SemaphoreType.DMA((7,)),
                pltpu.SemaphoreType.DMA((2, 2)),
                pltpu.SemaphoreType.DMA((2, 2)),
            ],
            compiler_params=pltpu.CompilerParams(
                collective_id=0, has_side_effects=True, vmem_limit_bytes=60 * 1024 * 1024
            ),
        )(
            features,
            gain_one.reshape(1, channels),
            shift_one.reshape(1, channels),
            conv_weight.reshape(3, 3, depth, own),
            gain_two.reshape(1, channels),
            shift_two.reshape(1, channels),
        )

    in_specs = (P("tm", "ha", "wa", None), P(), P(), P(None, None, None, None, "wa"), P(), P())
    return jax.shard_map(
        per_device, mesh=mesh, in_specs=in_specs, out_specs=P("tm", "ha", "wa", None), check_vma=False
    )
```

time: 53.6 us -> 43.4 us (0.81)
  local copies, waits for them, and re-layouts: 6.38 us -> 0.71 us
  Pallas kernels: 47 us -> 42.6 us
    unnamed x13 -> x1, local copies, waits for them, and re-layouts: 6.38 us -> 0.71 us
    pallas_call x1, Pallas kernels: 47 us -> 42.6 us  [per_device(): pl.pallas_call(functools.partial(kernel, nt, nh, nw), out_shape=pltpu.VME...]
where the time goes in v2:
time: 43.4 us; the launch traced here: 43.3 us
  Pallas kernels  42.6 us (98%)
  local copies, waits for them, and re-layouts  0.71 us (2%)
    pallas_call x1, Pallas kernels, per_device(): pl.pallas_call(functools.partial(kernel, nt, nh, nw), out_shape=pltpu.VME...  42.6 us

profile of v2, /device:TPU:1, one launch (start us, length us, event | category | flops | bytes accessed | tf_op | source)
XLA Modules:
  0.0 43.3 jit_solution(2877158665162124798)
XLA Ops:
  0.0 42.6 %shard_map.64 = bf16[1,2,128,512]{3,2,1,0:T(8,128)(2,1)S(1)} custom-call(bf16[1,2,128,512]{3,2,1,0:T(8,128)(2,1)} %feat_hbm.1, f32[1,512]{1,0:T(1,128)} %bitcast.6, f32[1,512]{1,0:T(1,128)} %bitcast.7, bf16[3,3,1536,128]{3,2,1,0:T(8,128)(2,1)} %bitcast.5, f32[1,512]{1,0:T(1,128)} %bitcast.8, f32[1,512]{1,0:T(1,128)} %bitcast.9), custom_call_target="tpu_custom_call" | custom-call | tf_op jit(solution)/shard_map/pallas_call | solution.py:387
  42.6 0.7 %copy.8 = bf16[1,2,128,512]{3,2,1,0:T(8,128)(2,1)} copy(bf16[1,2,128,512]{3,2,1,0:T(8,128)(2,1)S(1)} %shard_map.64) | data formatting | bytes 524288

commit v3 on v2

--- a/solution.py
+++ b/solution.py
@@ -56,7 +56,7 @@
     nt, nh, nw,
     feat_hbm, gain_one_hbm, shift_one_hbm, weight, gain_two_hbm, shift_two_hbm, out,
     feat, gain_one, shift_one, gain_two, shift_two,
-    message, blocks, acts, pair_a, pair_b, rim_pair, rim_last, acc, conv, conv_out, rim_out, rim_in, back,
+    message, blocks, acts, pairs, rim_pair, rim_last, acc, conv, conv_out, rim_out, rim_in, back,
     plane_one, line_one, line_two, plane_two, norm, norm_edge,
     input_sem, weight_sem, local_sem, send_sem, recv_sem, rim_send, rim_recv,
 ):
@@ -72,8 +72,7 @@
     rows = nt * span
     entries = 2 * columns
     everywhere = entries * plane * nh
-    slots = sorted(range(nw), key=lambda d: d % 2)
-    near = nw // 2
+    across = lax.rem(h, 2)
     offsets = [(a, b) for a in range(nt) for b in range(nw) if a or b]
     far_first = sorted(offsets, key=lambda d: -hops(d[0], nt) - hops(d[1], nw))
 
@@ -127,10 +126,10 @@
         ]
     for k in range(3):
         weight_copies += [
-            (weight.at[k, 1], pair_a.at[k, :, left_half]),
-            (weight.at[k, 0], pair_a.at[k, :, right_half]),
-            (weight.at[k, 2], pair_b.at[k, :, left_half]),
-            (weight.at[k, 1], pair_b.at[k, :, right_half]),
+            (weight.at[k, 1], pairs.at[0, k, :, left_half]),
+            (weight.at[k, 0], pairs.at[0, k, :, right_half]),
+            (weight.at[k, 2], pairs.at[1, k, :, left_half]),
+            (weight.at[k, 1], pairs.at[1, k, :, right_half]),
         ]
     weight_copies = [
         pltpu.make_async_copy(source, target, weight_sem.at[n])
@@ -178,14 +177,13 @@
     def all_sent(buffer, index):
         pltpu.make_async_copy(buffer, buffer, send_sem.at[index]).wait()
 
-    def send_blocks(stage):
+    def send_row(r, stage):
         for offset in far_first:
-            if (slots.index(offset[1]) >= near) == stage:
-                y, q = plane_peer(offset)
-                remote(feat.at[0, :, pl.ds(y * part, part), :], blocks.at[me], 1 + stage, (y, h, q)).start()
+            y, q = plane_peer(offset)
+            remote(feat.at[0, r, pl.ds(y * part, part), :], blocks.at[me, r], 1 + stage, (y, h, q)).start()
 
     line_loop(lambda j: remote(line_one.at[h], line_one.at[h], 3, (t, j, w)).start())
-    send_blocks(0)
+    send_row(across, 0)
     others = pl.ds(0, plane - 1)
     all_arrived(line_one.at[pl.ds(0, nh - 1)], 3)
     mean, deviation = combined(line_one[:, 0:4, :], line_one[:, 4:8, :], float(entries), 0)
@@ -195,7 +193,7 @@
     for offset in far_first:
         y, q = plane_peer(offset)
         remote(message.at[y], plane_one.at[me], 0, (y, h, q)).start()
-    send_blocks(1)
+    send_row(1 - across, 1)
     plane_one[me] = message[t]
     for copy in copy_in[1:]:
         copy.wait()
@@ -221,103 +219,88 @@
     last = lax.broadcasted_iota(jnp.int32, (part, channels), 0) == part - 1
     is_left = (lax.broadcasted_iota(jnp.int32, (16, LANES), 0) & 2) == 0
 
-    def activate(slot):
-        block = lax.rem(w + slots[slot], nw)
-        place = slice(slot * part, (slot + 1) * part)
-        left_from = jnp.where(t == 0, jnp.maximum(block - 1, 0), block)
-        right_from = jnp.where(t == nt - 1, jnp.minimum(block + 1, nw - 1), block)
-        left_end = jnp.logical_and(t == 0, block == 0)
-        right_end = jnp.logical_and(t == nt - 1, block == nw - 1)
-
-        def step(frame, carry):
-            edge = jnp.where(
-                is_left, plane_one[frame * nw + left_from, 8:24, :], plane_one[frame * nw + right_from, 8:24, :]
-            )
-            edge = silu((edge - norm_edge[0]) * norm_edge[1] + norm_edge[2])
-            for r in range(2):
-                raw = blocks[frame * nw + block, r].astype(jnp.float32)
+    def activate(r):
+        def step(pair, carry):
+            for j in (2 * pair, 2 * pair + 1):
+                frame, block = lax.div(j, nw), lax.rem(j, nw)
+                left_from = jnp.where(t == 0, jnp.maximum(block - 1, 0), block)
+                right_from = jnp.where(t == nt - 1, jnp.minimum(block + 1, nw - 1), block)
+                left_end = jnp.logical_and(t == 0, block == 0)
+                right_end = jnp.logical_and(t == nt - 1, block == nw - 1)
+                edge = jnp.where(
+                    is_left, plane_one[frame * nw + left_from, 8:24, :], plane_one[frame * nw + right_from, 8:24, :]
+                )
+                edge = silu((edge - norm_edge[0]) * norm_edge[1] + norm_edge[2])
+                raw = blocks[j, r].astype(jnp.float32)
                 middle = silu((raw - norm[0:1, :]) * norm[1:2, :] + norm[2:3, :])
-                left = jnp.concatenate([edge[4 * k + r : 4 * k + r + 1] for k in range(blocks_of)], axis=1)
-                right = jnp.concatenate([edge[4 * k + 2 + r : 4 * k + 3 + r] for k in range(blocks_of)], axis=1)
+                sides = [
+                    jnp.where(r == 0, edge[4 * k : 4 * k + 3], edge[4 * k + 1 : 4 * k + 4]) for k in range(blocks_of)
+                ]
+                left = jnp.concatenate([piece[0:1] for piece in sides], axis=1)
+                right = jnp.concatenate([piece[2:3] for piece in sides], axis=1)
                 left = jnp.where(left_end, middle[0:1, :], left)
                 right = jnp.where(right_end, middle[part - 1 : part, :], right)
-                before = jnp.where(first, left, pltpu.roll(middle, 1, 0)).astype(jnp.bfloat16)
-                after = jnp.where(last, right, pltpu.roll(middle, part - 1, 0)).astype(jnp.bfloat16)
-                middle = middle.astype(jnp.bfloat16)
-
-                def put(moment, before=before, middle=middle, after=after, r=r):
-                    acts[r, moment, place, 0:channels] = before
-                    acts[r, moment, place, channels : 2 * channels] = middle
-                    acts[r, moment, place, 2 * channels : 3 * channels] = after
-
-                put(frame + 2)
-
-                @pl.when(frame == 0)
-                def _(put=put):
-                    put(0)
-                    put(1)
-
+                before = jnp.where(first, left, pltpu.roll(middle, 1, 0))
+                after = jnp.where(last, right, pltpu.roll(middle, part - 1, 0))
+                place = pl.ds(pl.multiple_of(block * part, part), part)
+                acts[r, frame + 2, place, 0:channels] = before.astype(jnp.bfloat16)
+                acts[r, frame + 2, place, channels : 2 * channels] = middle.astype(jnp.bfloat16)
+                acts[r, frame + 2, place, 2 * channels : 3 * channels] = after.astype(jnp.bfloat16)
             return carry
 
-        lax.fori_loop(0, nt, step, 0)
-
-    def rim(side, stage, low, high):
-        count = high - low
-        window = acts[side, 2 : 2 + nt, low:high, :].reshape(nt * count, depth)
+        lax.fori_loop(0, plane // 2, step, 0)
+        initial = acts[r, 2]
+        acts[r, 0] = initial
+        acts[r, 1] = initial
+
+    def rim(side):
+        window = acts[side, 2 : 2 + nt].reshape(rows, depth)
         early = jnp.dot(window, rim_pair[side], preferred_element_type=jnp.float32)
         late = jnp.dot(window, rim_last[side], preferred_element_type=jnp.float32)
-        first_tap = early[:, 0:LANES].reshape(nt, count, LANES)
-        second_tap = early[:, LANES:].reshape(nt, count, LANES)
-        third_tap = late.reshape(nt, count, LANES)
+        first_tap = early[:, 0:LANES].reshape(nt, span, LANES)
+        second_tap = early[:, LANES:].reshape(nt, span, LANES)
+        third_tap = late.reshape(nt, span, LANES)
         for frame in range(nt):
             total = first_tap[max(frame - 2, 0)] + second_tap[max(frame - 1, 0)] + third_tap[frame]
-            rim_out[side, frame, low:high, :] = total.astype(jnp.bfloat16)
+            rim_out[side, frame] = total.astype(jnp.bfloat16)
         at_end = h == jnp.where(side == 0, 0, nh - 1)
 
         @pl.when(at_end)
         def _():
-            rim_in[side, :, low:high, :] = rim_out[side, :, low:high, :]
+            rim_in[side] = rim_out[side]
 
         @pl.when(jnp.logical_not(at_end))
         def _():
             pltpu.make_async_remote_copy(
-                src_ref=rim_out.at[side, :, low:high, :], dst_ref=rim_in.at[1 - side, :, low:high, :],
-                send_sem=rim_send.at[side, stage], recv_sem=rim_recv.at[1 - side, stage],
+                src_ref=rim_out.at[side], dst_ref=rim_in.at[1 - side],
+                send_sem=rim_send.at[side], recv_sem=rim_recv.at[1 - side],
                 device_id=(t, h - 1 + 2 * side, w), device_id_type=MESH,
             ).start()
 
-    across = lax.rem(h, 2)
-    for stage, (low, high) in enumerate(((0, near), (near, nw))):
+    acc[...] = jnp.zeros((rows, 2 * LANES), jnp.float32)
+    for stage in range(2):
+        r = across if stage == 0 else 1 - across
+        all_arrived(blocks.at[others, 0], 1 + stage)
         if stage == 0:
-            all_arrived(blocks.at[pl.ds(0, nt * near - 1)], 1)
             own_block.wait()
-        else:
-            all_arrived(blocks.at[pl.ds(0, nt * (nw - near))], 2)
-        for slot in range(low, high):
-            activate(slot)
-        rim(across, stage, low * part, high * part)
-        rim(1 - across, stage, low * part, high * part)
-
-    acc[...] = jnp.zeros((rows, 2 * LANES), jnp.float32)
-
-    def pair_step(k, carry):
-        acc[...] += jnp.dot(
-            acts[0, pl.ds(k, nt)].reshape(rows, depth), pair_a[k], preferred_element_type=jnp.float32
-        ) + jnp.dot(acts[1, pl.ds(k, nt)].reshape(rows, depth), pair_b[k], preferred_element_type=jnp.float32)
-        return carry
-
-    lax.fori_loop(0, 3, pair_step, 0)
+        activate(r)
+        rim(r)
+
+        def pair_step(k, carry, r=r):
+            acc[...] += jnp.dot(
+                acts[r, pl.ds(k, nt)].reshape(rows, depth), pairs[r, k], preferred_element_type=jnp.float32
+            )
+            return carry
+
+        lax.fori_loop(0, 3, pair_step, 0)
 
     for side in range(2):
         at_end = (h == 0) if side == 0 else (h == nh - 1)
 
         @pl.when(jnp.logical_not(at_end))
         def _(side=side):
-            for stage, (low, high) in enumerate(((0, near * part), (near * part, span))):
-                into = rim_in.at[side, :, low:high, :]
-                outof = rim_out.at[side, :, low:high, :]
-                pltpu.make_async_copy(into, into, rim_recv.at[side, stage]).wait()
-                pltpu.make_async_copy(outof, outof, rim_send.at[side, stage]).wait()
+            pltpu.make_async_copy(rim_in.at[side], rim_in.at[side], rim_recv.at[side]).wait()
+            pltpu.make_async_copy(rim_out.at[side], rim_out.at[side], rim_send.at[side]).wait()
 
     sums = jnp.zeros((1, LANES), jnp.float32)
     for r in range(2):
@@ -335,12 +318,14 @@
     line_two[h, 1:2, :] = deviation
     line_loop(lambda j: remote(line_two.at[h], line_two.at[h], 4, (t, j, w)).start())
 
+    def result_of(frame, block):
+        return conv_out.at[:, frame, pl.ds(pl.multiple_of(block * part, part), part), :]
+
     own_place = back.at[:, pl.ds(t * part, part), pl.ds(pl.multiple_of(w * LANES, LANES), LANES)]
     for offset in far_first:
         y, q = plane_peer(offset)
-        slot = slots.index(offset[1])
-        remote(conv_out.at[:, y, slot * part : (slot + 1) * part, :], own_place, 5, (y, h, q)).start()
-    own_back = pltpu.make_async_copy(conv_out.at[:, t, 0:part, :], own_place, local_sem.at[0])
+        remote(result_of(y, q), own_place, 5, (y, h, q)).start()
+    own_back = pltpu.make_async_copy(result_of(t, w), own_place, local_sem.at[0])
     own_back.start()
 
     all_arrived(line_two.at[pl.ds(0, nh - 1)], 4)
@@ -352,8 +337,8 @@
         y, q = plane_peer(offset)
         remote(plane_two.at[me], plane_two.at[me], 6, (y, h, q)).start()
     all_sent(plane_one.at[others], 0)
-    all_sent(blocks.at[pl.ds(0, nt * near - 1)], 1)
-    all_sent(blocks.at[pl.ds(0, nt * (nw - near))], 2)
+    all_sent(blocks.at[others, 0], 1)
+    all_sent(blocks.at[others, 0], 2)
     all_sent(line_one.at[pl.ds(0, nh - 1)], 3)
     all_sent(line_two.at[pl.ds(0, nh - 1)], 4)
     all_sent(blocks.at[others, :, :, 0:LANES], 5)
@@ -398,8 +383,7 @@
                 pltpu.VMEM((nt, 24, LANES), f32),
                 pltpu.VMEM((plane, 2, part, channels), bf16),
                 pltpu.VMEM((2, nt + 2, span, depth), bf16),
-                pltpu.VMEM((3, depth, 2 * own), bf16),
-                pltpu.VMEM((3, depth, 2 * own), bf16),
+                pltpu.VMEM((2, 3, depth, 2 * own), bf16),
                 pltpu.VMEM((2, depth, 2 * own), bf16),
                 pltpu.VMEM((2, depth, own), bf16),
                 pltpu.VMEM((rows, 2 * own), f32),
@@ -419,8 +403,8 @@
                 pltpu.SemaphoreType.DMA((1,)),
                 pltpu.SemaphoreType.DMA((7,)),
                 pltpu.SemaphoreType.DMA((7,)),
-                pltpu.SemaphoreType.DMA((2, 2)),
-                pltpu.SemaphoreType.DMA((2, 2)),
+                pltpu.SemaphoreType.DMA((2,)),
+                pltpu.SemaphoreType.DMA((2,)),
             ],
             compiler_params=pltpu.CompilerParams(
                 collective_id=0, has_side_effects=True, vmem_limit_bytes=60 * 1024 * 1024

time: 43.4 us -> 42.4 us (0.977)
  Pallas kernels: 42.6 us -> 41.6 us
    pallas_call x1, Pallas kernels: 42.6 us -> 41.6 us  [per_device(): pl.pallas_call(functools.partial(kernel, nt, nh, nw), out_shape=pltpu.VME...]
where the time goes in v3:
time: 42.4 us; the launch traced here: 42.3 us
  Pallas kernels  41.6 us (98%)
  local copies, waits for them, and re-layouts  0.71 us (2%)
    pallas_call x1, Pallas kernels, per_device(): pl.pallas_call(functools.partial(kernel, nt, nh, nw), out_shape=pltpu.VME...  41.6 us

profile of v3, /device:TPU:1, one launch (start us, length us, event | category | flops | bytes accessed | tf_op | source)
XLA Modules:
  0.0 42.3 jit_solution(12745678140006487037)
XLA Ops:
  0.0 41.6 %shard_map.64 = bf16[1,2,128,512]{3,2,1,0:T(8,128)(2,1)S(1)} custom-call(bf16[1,2,128,512]{3,2,1,0:T(8,128)(2,1)} %feat_hbm.1, f32[1,512]{1,0:T(1,128)} %bitcast.6, f32[1,512]{1,0:T(1,128)} %bitcast.7, bf16[3,3,1536,128]{3,2,1,0:T(8,128)(2,1)} %bitcast.5, f32[1,512]{1,0:T(1,128)} %bitcast.8, f32[1,512]{1,0:T(1,128)} %bitcast.9), custom_call_target="tpu_custom_call" | custom-call | tf_op jit(solution)/shard_map/pallas_call | solution.py:372
  41.6 0.7 %copy.8 = bf16[1,2,128,512]{3,2,1,0:T(8,128)(2,1)} copy(bf16[1,2,128,512]{3,2,1,0:T(8,128)(2,1)S(1)} %shard_map.64) | data formatting | bytes 524288

commit v4 on v3

--- a/solution.py
+++ b/solution.py
@@ -36,15 +36,18 @@
     return jnp.squeeze(mean, axis), total
 
 
-def group_norm_terms(mean, deviation, count, width):
+def grouped_terms(mean, deviation, count, width):
     group_mean = group_sum(mean, width) / width
     spread = mean - group_mean
-    group_var = group_sum(deviation + count * (spread * spread), width) / (count * width)
-    return group_mean, lax.rsqrt(group_var + EPS)
-
-
-def silu(v):
-    half = 0.5 * v
+    return group_mean, group_sum(deviation + count * (spread * spread), width)
+
+
+def group_norm_terms(mean, deviation, count, width):
+    group_mean, group_deviation = grouped_terms(mean, deviation, count, width)
+    return group_mean, lax.rsqrt(group_deviation / (count * width) + EPS)
+
+
+def silu_of_double(half):
     return half + half * jnp.tanh(half)
 
 
@@ -56,7 +59,7 @@
     nt, nh, nw,
     feat_hbm, gain_one_hbm, shift_one_hbm, weight, gain_two_hbm, shift_two_hbm, out,
     feat, gain_one, shift_one, gain_two, shift_two,
-    message, blocks, acts, pairs, rim_pair, rim_last, acc, conv, conv_out, rim_out, rim_in, back,
+    edge_out, blocks, edges, acts, pairs, rim_pair, rim_last, acc, conv, conv_out, rim_out, rim_in, back,
     plane_one, line_one, line_two, plane_two, norm, norm_edge,
     input_sem, weight_sem, local_sem, send_sem, recv_sem, rim_send, rim_recv,
 ):
@@ -146,9 +149,12 @@
     deviation = jnp.sum(centered * centered, axis=0, keepdims=True)
     pieces = [mean[:, k * LANES : (k + 1) * LANES] for k in range(blocks_of)]
     pieces += [jnp.zeros((1, LANES), jnp.float32)] * (4 - blocks_of)
-    pieces += [deviation[:, k * LANES : (k + 1) * LANES] for k in range(blocks_of)]
+    means = jnp.concatenate(pieces, axis=0)
+    pieces = [deviation[:, k * LANES : (k + 1) * LANES] for k in range(blocks_of)]
     pieces += [jnp.zeros((1, LANES), jnp.float32)] * (4 - blocks_of)
-    local_terms = jnp.concatenate(pieces, axis=0)
+    line_one[h] = jnp.concatenate(
+        grouped_terms(means, jnp.concatenate(pieces, axis=0), float(entries), float(width)), axis=0
+    )
     for y in range(nt):
         left = (y * part - 1) % columns
         right = (y * part + part) % columns
@@ -157,8 +163,8 @@
         )
         pieces = [four[:, k * LANES : (k + 1) * LANES] for k in range(blocks_of)]
         pieces += [jnp.zeros((4, LANES), jnp.float32)] * (4 - blocks_of)
-        message[y, 8:24, :] = jnp.concatenate(pieces, axis=0)
-    line_one[h] = local_terms
+        edge_out[y] = jnp.concatenate(pieces, axis=0).astype(jnp.bfloat16)
+    edges[me] = edge_out[t]
 
     own_block = pltpu.make_async_copy(feat.at[0, :, pl.ds(t * part, part), :], blocks.at[me], local_sem.at[0])
     own_block.start()
@@ -184,30 +190,31 @@
 
     line_loop(lambda j: remote(line_one.at[h], line_one.at[h], 3, (t, j, w)).start())
     send_row(across, 0)
+    for offset in far_first:
+        y, q = plane_peer(offset)
+        remote(edge_out.at[y], edges.at[me], 7, (y, h, q)).start()
     others = pl.ds(0, plane - 1)
     all_arrived(line_one.at[pl.ds(0, nh - 1)], 3)
-    mean, deviation = combined(line_one[:, 0:4, :], line_one[:, 4:8, :], float(entries), 0)
-    combined_terms = jnp.concatenate([mean, deviation], axis=0)
-    for y in range(nt):
-        message[y, 0:8, :] = combined_terms
+    mean, deviation = combined(line_one[:, 0:4, :], line_one[:, 4:8, :], float(entries * width), 0)
+    plane_one[me] = jnp.concatenate([mean, deviation], axis=0)
     for offset in far_first:
         y, q = plane_peer(offset)
-        remote(message.at[y], plane_one.at[me], 0, (y, h, q)).start()
+        remote(plane_one.at[me], plane_one.at[me], 0, (y, h, q)).start()
     send_row(1 - across, 1)
-    plane_one[me] = message[t]
     for copy in copy_in[1:]:
         copy.wait()
     for copy in weight_copies:
         copy.wait()
     all_arrived(plane_one.at[others], 0)
-    mean, deviation = combined(plane_one[:, 0:4, :], plane_one[:, 4:8, :], float(entries * nh), 0)
-    mean, inverse = group_norm_terms(mean, deviation, float(everywhere), float(width))
+    mean, deviation = combined(plane_one[:, 0:4, :], plane_one[:, 4:8, :], float(entries * width * nh), 0)
+    inverse = lax.rsqrt(deviation / float(everywhere * width) + EPS)
     wide_mean = jnp.concatenate(lane_blocks(mean[0:blocks_of]), axis=1)
-    wide_scale = jnp.concatenate(lane_blocks(inverse[0:blocks_of]), axis=1) * gain_one[...]
+    wide_scale = jnp.concatenate(lane_blocks(inverse[0:blocks_of]), axis=1) * (0.5 * gain_one[...])
+    wide_shift = 0.5 * shift_one[...]
     norm[0:1, :] = wide_mean
     norm[1:2, :] = wide_scale
-    norm[2:3, :] = shift_one[...]
-    for n, vector in enumerate((wide_mean, wide_scale, shift_one[...])):
+    norm[2:3, :] = wide_shift
+    for n, vector in enumerate((wide_mean, wide_scale, wide_shift)):
         for k in range(blocks_of):
             norm_edge[n, 4 * k : 4 * k + 4, :] = jnp.broadcast_to(
                 vector[:, k * LANES : (k + 1) * LANES], (4, LANES)
@@ -215,8 +222,8 @@
         if blocks_of < 4:
             norm_edge[n, 4 * blocks_of :, :] = jnp.zeros((16 - 4 * blocks_of, LANES), jnp.float32)
 
-    first = lax.broadcasted_iota(jnp.int32, (part, channels), 0) == 0
-    last = lax.broadcasted_iota(jnp.int32, (part, channels), 0) == part - 1
+    sublane = lax.broadcasted_iota(jnp.int32, (8, channels), 0)
+    first, last = sublane == 0, sublane == 7
     is_left = (lax.broadcasted_iota(jnp.int32, (16, LANES), 0) & 2) == 0
 
     def activate(r):
@@ -228,11 +235,13 @@
                 left_end = jnp.logical_and(t == 0, block == 0)
                 right_end = jnp.logical_and(t == nt - 1, block == nw - 1)
                 edge = jnp.where(
-                    is_left, plane_one[frame * nw + left_from, 8:24, :], plane_one[frame * nw + right_from, 8:24, :]
+                    is_left,
+                    edges[frame * nw + left_from].astype(jnp.float32),
+                    edges[frame * nw + right_from].astype(jnp.float32),
                 )
-                edge = silu((edge - norm_edge[0]) * norm_edge[1] + norm_edge[2])
+                edge = silu_of_double((edge - norm_edge[0]) * norm_edge[1] + norm_edge[2])
                 raw = blocks[j, r].astype(jnp.float32)
-                middle = silu((raw - norm[0:1, :]) * norm[1:2, :] + norm[2:3, :])
+                middle = silu_of_double((raw - norm[0:1, :]) * norm[1:2, :] + norm[2:3, :])
                 sides = [
                     jnp.where(r == 0, edge[4 * k : 4 * k + 3], edge[4 * k + 1 : 4 * k + 4]) for k in range(blocks_of)
                 ]
@@ -240,26 +249,26 @@
                 right = jnp.concatenate([piece[2:3] for piece in sides], axis=1)
                 left = jnp.where(left_end, middle[0:1, :], left)
                 right = jnp.where(right_end, middle[part - 1 : part, :], right)
-                before = jnp.where(first, left, pltpu.roll(middle, 1, 0))
-                after = jnp.where(last, right, pltpu.roll(middle, part - 1, 0))
+                before = pltpu.roll(middle, 1, 0)
+                before = jnp.concatenate([jnp.where(first, left, before[0:8]), before[8:]], axis=0)
+                after = pltpu.roll(middle, part - 1, 0)
+                after = jnp.concatenate([after[: part - 8], jnp.where(last, right, after[part - 8 :])], axis=0)
                 place = pl.ds(pl.multiple_of(block * part, part), part)
-                acts[r, frame + 2, place, 0:channels] = before.astype(jnp.bfloat16)
-                acts[r, frame + 2, place, channels : 2 * channels] = middle.astype(jnp.bfloat16)
-                acts[r, frame + 2, place, 2 * channels : 3 * channels] = after.astype(jnp.bfloat16)
+                acts[r, frame, place, 0:channels] = before.astype(jnp.bfloat16)
+                acts[r, frame, place, channels : 2 * channels] = middle.astype(jnp.bfloat16)
+                acts[r, frame, place, 2 * channels : 3 * channels] = after.astype(jnp.bfloat16)
             return carry
 
         lax.fori_loop(0, plane // 2, step, 0)
-        initial = acts[r, 2]
-        acts[r, 0] = initial
-        acts[r, 1] = initial
+
+    def product(r, frames, taps):
+        window = acts[r, 0:frames].reshape(frames * span, depth)
+        return jnp.dot(window, taps, preferred_element_type=jnp.float32).reshape(frames, span, taps.shape[1])
 
     def rim(side):
-        window = acts[side, 2 : 2 + nt].reshape(rows, depth)
-        early = jnp.dot(window, rim_pair[side], preferred_element_type=jnp.float32)
-        late = jnp.dot(window, rim_last[side], preferred_element_type=jnp.float32)
-        first_tap = early[:, 0:LANES].reshape(nt, span, LANES)
-        second_tap = early[:, LANES:].reshape(nt, span, LANES)
-        third_tap = late.reshape(nt, span, LANES)
+        early = product(side, nt - 1, rim_pair[side])
+        third_tap = product(side, nt, rim_last[side])
+        first_tap, second_tap = early[:, :, 0:LANES], early[:, :, LANES:]
         for frame in range(nt):
             total = first_tap[max(frame - 2, 0)] + second_tap[max(frame - 1, 0)] + third_tap[frame]
             rim_out[side, frame] = total.astype(jnp.bfloat16)
@@ -277,22 +286,20 @@
                 device_id=(t, h - 1 + 2 * side, w), device_id_type=MESH,
             ).start()
 
-    acc[...] = jnp.zeros((rows, 2 * LANES), jnp.float32)
     for stage in range(2):
         r = across if stage == 0 else 1 - across
         all_arrived(blocks.at[others, 0], 1 + stage)
         if stage == 0:
             own_block.wait()
+            all_arrived(edges.at[others], 7)
         activate(r)
         rim(r)
 
-        def pair_step(k, carry, r=r):
-            acc[...] += jnp.dot(
-                acts[r, pl.ds(k, nt)].reshape(rows, depth), pairs[r, k], preferred_element_type=jnp.float32
-            )
-            return carry
-
-        lax.fori_loop(0, 3, pair_step, 0)
+        for k in range(3):
+            made = product(r, nt - 2 + k, pairs[r, k])
+            for frame in range(nt):
+                part_sum = made[max(frame - 2 + k, 0)]
+                acc[frame] = part_sum if stage == 0 and k == 0 else acc[frame] + part_sum
 
     for side in range(2):
         at_end = (h == 0) if side == 0 else (h == nh - 1)
@@ -304,10 +311,10 @@
 
     sums = jnp.zeros((1, LANES), jnp.float32)
     for r in range(2):
-        total = acc[:, r * LANES : (r + 1) * LANES] + rim_in[r].reshape(rows, LANES).astype(jnp.float32)
-        conv[r] = total
-        conv_out[r] = total.astype(jnp.bfloat16).reshape(nt, span, LANES)
-        sums = sums + jnp.sum(total, axis=0, keepdims=True)
+        total = acc[:, :, r * LANES : (r + 1) * LANES] + rim_in[r].astype(jnp.float32)
+        conv[r] = total.reshape(rows, LANES)
+        conv_out[r] = total.astype(jnp.bfloat16)
+        sums = sums + jnp.sum(total.reshape(rows, LANES), axis=0, keepdims=True)
     mean = sums / (2 * rows)
     deviation = jnp.zeros((1, LANES), jnp.float32)
     for r in range(2):
@@ -337,6 +344,7 @@
         y, q = plane_peer(offset)
         remote(plane_two.at[me], plane_two.at[me], 6, (y, h, q)).start()
     all_sent(plane_one.at[others], 0)
+    all_sent(edges.at[others], 7)
     all_sent(blocks.at[others, 0], 1)
     all_sent(blocks.at[others, 0], 2)
     all_sent(line_one.at[pl.ds(0, nh - 1)], 3)
@@ -349,10 +357,10 @@
     mean, deviation = combined(gathered[:, :, 0, :], gathered[:, :, 1, :], float(2 * rows * nh), 0)
     mean, inverse = group_norm_terms(mean, deviation, float(everywhere), float(width))
     norm[0:1, :] = jnp.concatenate(lane_blocks(mean), axis=1)
-    norm[1:2, :] = jnp.concatenate(lane_blocks(inverse), axis=1) * gain_two[...]
-    norm[2:3, :] = shift_two[...]
+    norm[1:2, :] = jnp.concatenate(lane_blocks(inverse), axis=1) * (0.5 * gain_two[...])
+    norm[2:3, :] = 0.5 * shift_two[...]
     for r in range(2):
-        out[0, r] = silu(
+        out[0, r] = silu_of_double(
             (back[r].astype(jnp.float32) - norm[0:1, :]) * norm[1:2, :] + norm[2:3, :]
         ).astype(jnp.bfloat16)
     all_sent(plane_two.at[others], 6)
@@ -380,19 +388,20 @@
                 pltpu.VMEM((1, channels), f32),
                 pltpu.VMEM((1, channels), f32),
                 pltpu.VMEM((1, channels), f32),
-                pltpu.VMEM((nt, 24, LANES), f32),
+                pltpu.VMEM((nt, 16, LANES), bf16),
                 pltpu.VMEM((plane, 2, part, channels), bf16),
-                pltpu.VMEM((2, nt + 2, span, depth), bf16),
+                pltpu.VMEM((plane, 16, LANES), bf16),
+                pltpu.VMEM((2, nt, span, depth), bf16),
                 pltpu.VMEM((2, 3, depth, 2 * own), bf16),
                 pltpu.VMEM((2, depth, 2 * own), bf16),
                 pltpu.VMEM((2, depth, own), bf16),
-                pltpu.VMEM((rows, 2 * own), f32),
+                pltpu.VMEM((nt, span, 2 * own), f32),
                 pltpu.VMEM((2, rows, own), f32),
                 pltpu.VMEM((2, nt, span, own), bf16),
                 pltpu.VMEM((2, nt, span, own), bf16),
                 pltpu.VMEM((2, nt, span, own), bf16),
                 pltpu.VMEM((2, columns, channels), bf16),
-                pltpu.VMEM((plane, 24, LANES), f32),
+                pltpu.VMEM((plane, 8, LANES), f32),
                 pltpu.VMEM((nh, 8, LANES), f32),
                 pltpu.VMEM((nh, 8, LANES), f32),
                 pltpu.VMEM((plane, 8, LANES), f32),
@@ -401,8 +410,8 @@
                 pltpu.SemaphoreType.DMA((5,)),
                 pltpu.SemaphoreType.DMA((18,)),
                 pltpu.SemaphoreType.DMA((1,)),
-                pltpu.SemaphoreType.DMA((7,)),
-                pltpu.SemaphoreType.DMA((7,)),
+                pltpu.SemaphoreType.DMA((8,)),
+                pltpu.SemaphoreType.DMA((8,)),
                 pltpu.SemaphoreType.DMA((2,)),
                 pltpu.SemaphoreType.DMA((2,)),
             ],

time: 42.4 us -> 41.3 us (0.974)
  Pallas kernels: 41.6 us -> 40.5 us
    pallas_call x1, Pallas kernels: 41.6 us -> 40.5 us  [per_device(): pl.pallas_call(functools.partial(kernel, nt, nh, nw), out_shape=pltpu.VME...]
where the time goes in v4:
time: 41.3 us; the launch traced here: 41.2 us
  Pallas kernels  40.5 us (98%)
  local copies, waits for them, and re-layouts  0.71 us (2%)
    pallas_call x1, Pallas kernels, per_device(): pl.pallas_call(functools.partial(kernel, nt, nh, nw), out_shape=pltpu.VME...  40.5 us

profile of v4, /device:TPU:1, one launch (start us, length us, event | category | flops | bytes accessed | tf_op | source)
XLA Modules:
  0.0 41.2 jit_solution(7825717774121602887)
XLA Ops:
  0.0 40.5 %shard_map.64 = bf16[1,2,128,512]{3,2,1,0:T(8,128)(2,1)S(1)} custom-call(bf16[1,2,128,512]{3,2,1,0:T(8,128)(2,1)} %feat_hbm.1, f32[1,512]{1,0:T(1,128)} %bitcast.6, f32[1,512]{1,0:T(1,128)} %bitcast.7, bf16[3,3,1536,128]{3,2,1,0:T(8,128)(2,1)} %bitcast.5, f32[1,512]{1,0:T(1,128)} %bitcast.8, f32[1,512]{1,0:T(1,128)} %bitcast.9), custom_call_target="tpu_custom_call" | custom-call | tf_op jit(solution)/shard_map/pallas_call | solution.py:380
  40.5 0.7 %copy.8 = bf16[1,2,128,512]{3,2,1,0:T(8,128)(2,1)} copy(bf16[1,2,128,512]{3,2,1,0:T(8,128)(2,1)S(1)} %shard_map.64) | data formatting | bytes 524288

commit v5 on v4

--- a/solution.py
+++ b/solution.py
@@ -42,11 +42,6 @@
     return group_mean, group_sum(deviation + count * (spread * spread), width)
 
 
-def group_norm_terms(mean, deviation, count, width):
-    group_mean, group_deviation = grouped_terms(mean, deviation, count, width)
-    return group_mean, lax.rsqrt(group_deviation / (count * width) + EPS)
-
-
 def silu_of_double(half):
     return half + half * jnp.tanh(half)
 
@@ -57,9 +52,9 @@
 
 def kernel(
     nt, nh, nw,
-    feat_hbm, gain_one_hbm, shift_one_hbm, weight, gain_two_hbm, shift_two_hbm, out,
+    feat_hbm, gain_one_hbm, shift_one_hbm, weight, gain_two_hbm, shift_two_hbm, back, mean_two, scale_two, half_shift,
     feat, gain_one, shift_one, gain_two, shift_two,
-    edge_out, blocks, edges, acts, pairs, rim_pair, rim_last, acc, conv, conv_out, rim_out, rim_in, back,
+    edge_out, blocks, edges, acts, pairs, rim_pair, rim_last, acc, conv_out, rim_out, rim_in,
     plane_one, line_one, line_two, plane_two, norm, norm_edge,
     input_sem, weight_sem, local_sem, send_sem, recv_sem, rim_send, rim_recv,
 ):
@@ -228,7 +223,7 @@
 
     def activate(r):
         def step(pair, carry):
-            for j in (2 * pair, 2 * pair + 1):
+            for j in (4 * pair, 4 * pair + 1, 4 * pair + 2, 4 * pair + 3):
                 frame, block = lax.div(j, nw), lax.rem(j, nw)
                 left_from = jnp.where(t == 0, jnp.maximum(block - 1, 0), block)
                 right_from = jnp.where(t == nt - 1, jnp.minimum(block + 1, nw - 1), block)
@@ -259,7 +254,7 @@
                 acts[r, frame, place, 2 * channels : 3 * channels] = after.astype(jnp.bfloat16)
             return carry
 
-        lax.fori_loop(0, plane // 2, step, 0)
+        lax.fori_loop(0, plane // 4, step, 0)
 
     def product(r, frames, taps):
         window = acts[r, 0:frames].reshape(frames * span, depth)
@@ -309,20 +304,23 @@
             pltpu.make_async_copy(rim_in.at[side], rim_in.at[side], rim_recv.at[side]).wait()
             pltpu.make_async_copy(rim_out.at[side], rim_out.at[side], rim_send.at[side]).wait()
 
+    pivot = acc[0, 0:1, 0:LANES] + rim_in[0, 0, 0:16].astype(jnp.float32)[0:1]
     sums = jnp.zeros((1, LANES), jnp.float32)
+    squares = jnp.zeros((1, LANES), jnp.float32)
     for r in range(2):
         total = acc[:, :, r * LANES : (r + 1) * LANES] + rim_in[r].astype(jnp.float32)
-        conv[r] = total.reshape(rows, LANES)
         conv_out[r] = total.astype(jnp.bfloat16)
-        sums = sums + jnp.sum(total.reshape(rows, LANES), axis=0, keepdims=True)
-    mean = sums / (2 * rows)
-    deviation = jnp.zeros((1, LANES), jnp.float32)
-    for r in range(2):
-        centered = conv[r] - mean
-        deviation = deviation + jnp.sum(centered * centered, axis=0, keepdims=True)
+        moved = total.reshape(rows, LANES) - pivot
+        sums = sums + jnp.sum(moved, axis=0, keepdims=True)
+        squares = squares + jnp.sum(moved * moved, axis=0, keepdims=True)
+    mean = pivot + sums / (2 * rows)
+    deviation = jnp.maximum(squares - sums * (sums / (2 * rows)), 0.0)
     line_two[h] = jnp.zeros((8, LANES), jnp.float32)
-    line_two[h, 0:1, :] = mean
-    line_two[h, 1:2, :] = deviation
+    group_mean, group_deviation = grouped_terms(
+        jnp.broadcast_to(mean, (8, LANES)), jnp.broadcast_to(deviation, (8, LANES)), float(2 * rows), float(width)
+    )
+    line_two[h, 0:1, :] = group_mean[0:1]
+    line_two[h, 1:2, :] = group_deviation[0:1]
     line_loop(lambda j: remote(line_two.at[h], line_two.at[h], 4, (t, j, w)).start())
 
     def result_of(frame, block):
@@ -336,7 +334,7 @@
     own_back.start()
 
     all_arrived(line_two.at[pl.ds(0, nh - 1)], 4)
-    mean, deviation = combined(line_two[:, 0:1, :], line_two[:, 1:2, :], float(2 * rows), 0)
+    mean, deviation = combined(line_two[:, 0:1, :], line_two[:, 1:2, :], float(2 * rows * width), 0)
     plane_two[me] = jnp.zeros((8, LANES), jnp.float32)
     plane_two[me, 0:1, :] = mean
     plane_two[me, 1:2, :] = deviation
@@ -354,15 +352,11 @@
     own_back.wait()
     all_arrived(plane_two.at[others], 6)
     gathered = plane_two[...].reshape(nt, nw, 8, LANES)
-    mean, deviation = combined(gathered[:, :, 0, :], gathered[:, :, 1, :], float(2 * rows * nh), 0)
-    mean, inverse = group_norm_terms(mean, deviation, float(everywhere), float(width))
-    norm[0:1, :] = jnp.concatenate(lane_blocks(mean), axis=1)
-    norm[1:2, :] = jnp.concatenate(lane_blocks(inverse), axis=1) * (0.5 * gain_two[...])
-    norm[2:3, :] = 0.5 * shift_two[...]
-    for r in range(2):
-        out[0, r] = silu_of_double(
-            (back[r].astype(jnp.float32) - norm[0:1, :]) * norm[1:2, :] + norm[2:3, :]
-        ).astype(jnp.bfloat16)
+    mean, deviation = combined(gathered[:, :, 0, :], gathered[:, :, 1, :], float(2 * rows * nh * width), 0)
+    inverse = lax.rsqrt(deviation / float(everywhere * width) + EPS)
+    mean_two[...] = jnp.concatenate(lane_blocks(mean), axis=1)
+    scale_two[...] = jnp.concatenate(lane_blocks(inverse), axis=1) * (0.5 * gain_two[...])
+    half_shift[...] = 0.5 * shift_two[...]
     all_sent(plane_two.at[others], 6)
 
 
@@ -377,11 +371,11 @@
         rows = nt * span
         vmem = pl.BlockSpec(memory_space=pltpu.VMEM)
         bf16, f32 = jnp.bfloat16, jnp.float32
-        return pl.pallas_call(
+        back, mean, scale, shift = pl.pallas_call(
             functools.partial(kernel, nt, nh, nw),
-            out_shape=pltpu.VMEM(features.shape, bf16),
+            out_shape=(pltpu.VMEM((2, columns, channels), bf16), *[pltpu.VMEM((1, channels), f32)] * 3),
             in_specs=[pl.BlockSpec(memory_space=pltpu.HBM)] * 6,
-            out_specs=vmem,
+            out_specs=(vmem,) * 4,
             scratch_shapes=[
                 pltpu.VMEM(features.shape, bf16),
                 pltpu.VMEM((1, channels), f32),
@@ -396,11 +390,9 @@
                 pltpu.VMEM((2, depth, 2 * own), bf16),
                 pltpu.VMEM((2, depth, own), bf16),
                 pltpu.VMEM((nt, span, 2 * own), f32),
-                pltpu.VMEM((2, rows, own), f32),
                 pltpu.VMEM((2, nt, span, own), bf16),
                 pltpu.VMEM((2, nt, span, own), bf16),
                 pltpu.VMEM((2, nt, span, own), bf16),
-                pltpu.VMEM((2, columns, channels), bf16),
                 pltpu.VMEM((plane, 8, LANES), f32),
                 pltpu.VMEM((nh, 8, LANES), f32),
                 pltpu.VMEM((nh, 8, LANES), f32),
@@ -426,6 +418,8 @@
             gain_two.reshape(1, channels),
             shift_two.reshape(1, channels),
         )
+        result = silu_of_double((back.astype(f32) - mean) * scale + shift)
+        return result.astype(bf16)[None]
 
     in_specs = (P("tm", "ha", "wa", None), P(), P(), P(None, None, None, None, "wa"), P(), P())
     return jax.shard_map(

time: 41.3 us -> 41.3 us (level)
  other arithmetic: 0 us -> 0.84 us
  local copies, waits for them, and re-layouts: 0.71 us -> 0 us
    broadcast_in_dim x0 -> x1, other arithmetic: none -> 0.84 us  [per_device(): return result.astype(bf16)[None]]
    unnamed x1 -> x0, local copies, waits for them, and re-layouts: 0.71 us -> none
where the time goes in v5:
time: 41.3 us; the launch traced here: 41.2 us
  Pallas kernels  40.3 us (98%)
  other arithmetic  0.84 us (2%)
    pallas_call x1, Pallas kernels, per_device(): pl.pallas_call(functools.partial(kernel, nt, nh, nw), out_shape=(pltpu.VM...  40.3 us
    broadcast_in_dim x1, other arithmetic, per_device(): return result.astype(bf16)[None]  0.84 us

profile of v5, /device:TPU:1, one launch (start us, length us, event | category | flops | bytes accessed | tf_op | source)
XLA Modules:
  0.0 41.2 jit_solution(9808382285921051320)
XLA Ops:
  0.0 40.3 %shard_map.64 = (bf16[2,128,512]{2,1,0:T(8,128)(2,1)S(1)}, f32[1,512]{1,0:T(1,128)S(1)}, f32[1,512]{1,0:T(1,128)S(1)}, f32[1,512]{1,0:T(1,128)S(1)}) custom-call(bf16[1,2,128,512]{3,2,1,0:T(8,128)(2,1)} %feat_hbm.1, f32[1,512]{1,0:T(1,128)} %bitcast.14, f32[1,512]{1,0:T(1,128)} %bitcast.15, bf16[3,3,1536,128]{3,2,1,0:T(8,128)(2,1)} %bitcast.13, ...), custom_call_target="tpu_custom_call" | custom-call | tf_op jit(solution)/shard_map/pallas_call | solution.py:374
  40.3 0.8 %fusion.1 = bf16[1,2,128,512]{3,2,1,0:T(8,128)(2,1)} fusion(bf16[2,128,512]{2,1,0:T(8,128)(2,1)S(1)} %get-tuple-element.9, f32[512]{0:T(512)S(1)} %bitcast.12, f32[512]{0:T(512)S(1)} %bitcast.11, f32[512]{0:T(512)S(1)} %bitcast.10), kind=kLoop, calls=%fused_computation.2 | loop fusion | flops 917504 | bytes 530432 | tf_op jit(solution)/shard_map/broadcast_in_dim | solution.py:422
